TPU v7x, 32 devices: a whole 2x2x4 slice. The times are simulated.
32 devices in a mesh: dp: 8 (over z, y), row: 2 (over x), col: 2 (over core).
Axes of the slice: x: 2, y: 2, z: 4, core: 2. Of those that a mesh axis runs over, the one named last changes fastest.
Arguments:
- inputs: bfloat16 [48, 512, 960], P('dp', 'col', 'row'), may hold values from -6 to 6
- segments: int32 [48, 512], P('dp'), may hold values from 0 to 2, as said below
- positions: int32 [48, 512], P('dp'), may hold values from 0 to 511, as said below
- gain_first: float32 [960], P('row'), may hold values from 0.5 to 1.5
- query_weight: bfloat16 [960, 960], P(('row', 'col')), may hold values from -0.1875 to 0.1875
- key_weight: bfloat16 [960, 320], P(('row', 'col')), may hold values from -0.1875 to 0.1875
- value_weight: bfloat16 [960, 320], P(('row', 'col')), may hold values from -0.1875 to 0.1875
- output_weight: bfloat16 [960, 960], P(('row', 'col')), may hold values from -0.5 to 0.5
- gain_second: float32 [960], P('row'), may hold values from 0.5 to 1.5
- gate_weight: bfloat16 [960, 2560], P('row', 'col'), may hold values from -0.1875 to 0.1875
- up_weight: bfloat16 [960, 2560], P('row', 'col'), may hold values from -0.1875 to 0.1875
- down_weight: bfloat16 [2560, 960], P('col', 'row'), may hold values from -0.25 to 0.25
- cotangent: bfloat16 [48, 512, 960], P('dp', 'col', 'row'), may hold values from -6 to 6
Outputs:
- layer_out: bfloat16 [48, 512, 960], P('dp', 'col', 'row')
- input_grad: float32 [48, 512, 960], P('dp', 'col', 'row')
- gain_first_grad: float32 [960], P('row')
- query_grad: float32 [960, 960], P(('row', 'col'))
- key_grad: float32 [960, 320], P(('row', 'col'))
- value_grad: float32 [960, 320], P(('row', 'col'))
- output_grad: float32 [960, 960], P(('row', 'col'))
- gain_second_grad: float32 [960], P('row')
- gate_grad: float32 [960, 2560], P('row', 'col')
- up_grad: float32 [960, 2560], P('row', 'col')
- down_grad: float32 [2560, 960], P('col', 'row')
Inputs may be any that keep to these rules, and one draw needn't show every extreme that they name: `segments`: within a sequence the segment numbers start at 0 and never fall; in the 6 sequences of each index of dp one sequence is a single segment and another holds three. `positions`: each token's offset from the first token of its segment in its sequence.
All inputs are finite; a program needn't handle non-finite values.
Results may differ from a plain program's by a relative error of at most 0.02.
Values may be sent and summed in bfloat16 or wider, within the bound.
A program may use at most 192 MiB of HBM per device.

v0:
```python
import jax
import jax.numpy as jnp
from jax import lax
from jax.sharding import PartitionSpec as P

D = 960
QH = 15
KH = 5
HD = 64
QD = 960
KD = 320


eps_norm = 1e-05
rope_base = 10000.0
masked_value = -1e30


def row_total(values):
    return lax.psum(values, "row")


def to_tokens(values):
    return lax.all_to_all(values, "row", split_axis=1, concat_axis=2, tiled=True)


def to_features(values):
    return lax.all_to_all(values, "row", split_axis=2, concat_axis=1, tiled=True)


def col_rows(values, row_fn):
    return row_fn(lax.all_gather(values, "col", axis=0, tiled=True), jnp.int32(0))


def col_sums(term_fn, row_count):
    return lax.psum_scatter(
        term_fn(jnp.int32(0), lax.axis_size("col") * row_count),
        "col",
        scatter_dimension=0,
        tiled=True,
    )


def norm_apply(values, gain):
    sq_total = row_total(jnp.sum(values * values, axis=-1))
    inv_root = lax.rsqrt(sq_total[..., None] / D + eps_norm)
    return ((values * inv_root * gain).astype(jnp.bfloat16), inv_root)


def norm_back(values, inv_root, gain, grad_normed):
    weighted = grad_normed * gain
    cross = row_total(jnp.sum(weighted * values, axis=-1))
    grad_values = inv_root * weighted - values * inv_root**3 * cross[..., None] / D
    gain_part = jnp.sum(grad_normed * values * inv_root, axis=(0, 1))
    return (grad_values, gain_part)


def rotary(pos_rows):
    frequency = rope_base ** (-(jnp.arange(HD // 2, dtype=jnp.float32) * 2.0 / HD))
    angle_grid = pos_rows.astype(jnp.float32)[..., None] * frequency
    return (jnp.cos(angle_grid)[:, :, None, :], jnp.sin(angle_grid)[:, :, None, :])


def rotate(values, cosine, sine_term):
    half_dim = values.shape[-1] // 2
    lead_half = values[..., :half_dim]
    tail_half = values[..., half_dim:]
    return jnp.concatenate(
        [lead_half * cosine - tail_half * sine_term, tail_half * cosine + lead_half * sine_term],
        axis=-1,
    )


def unrotate(grads, cosine, sine_term):
    half_dim = grads.shape[-1] // 2
    lead_half = grads[..., :half_dim]
    tail_half = grads[..., half_dim:]
    return jnp.concatenate(
        [lead_half * cosine + tail_half * sine_term, tail_half * cosine - lead_half * sine_term],
        axis=-1,
    )


def masked_scores(query_grp, key_rows, allowed):
    scores = jnp.einsum(
        "sqhgd,skhd->shgqk", query_grp, key_rows, preferred_element_type=jnp.float32
    ) * HD ** (-0.5)
    return jnp.where(allowed[:, None, None], scores, masked_value)


def split_kv(kv_rows, seq_count, length):
    key_rows = kv_rows[..., :KD].reshape(seq_count, length, KH, HD)
    value_rows = kv_rows[..., KD:].reshape(seq_count, length, KH, HD)
    return (key_rows, value_rows)


def local(
    inputs,
    segments,
    positions,
    gain_first,
    query_weight,
    key_weight,
    value_weight,
    output_weight,
    gain_second,
    gate_weight,
    up_weight,
    down_weight,
    cotangent,
):
    seq_count, half_len, half_width = inputs.shape
    length = segments.shape[1]
    row_size = lax.axis_size("row")
    col_size = lax.axis_size("col")
    quarter = length // (row_size * col_size)
    own_rows = seq_count * quarter
    row_index = lax.axis_index("row")
    col_index = lax.axis_index("col")
    query_full, key_full, value_full, output_full = (
        lax.all_gather(query_weight, ("row", "col"), axis=0, tiled=True),
        lax.all_gather(key_weight, ("row", "col"), axis=0, tiled=True),
        lax.all_gather(value_weight, ("row", "col"), axis=0, tiled=True),
        lax.all_gather(output_weight, ("row", "col"), axis=0, tiled=True),
    )
    query_start = (col_index * row_size + row_index) * quarter
    query_pos = lax.dynamic_slice_in_dim(positions, query_start, quarter, 1)
    query_seg = lax.dynamic_slice_in_dim(segments, query_start, quarter, 1)
    key_seg = (
        segments.reshape(seq_count, col_size, row_size, quarter)
        .transpose(0, 2, 1, 3)
        .reshape(seq_count, length)
    )
    key_order = (
        jnp.arange(length, dtype=jnp.int32)
        .reshape(col_size, row_size, quarter)
        .transpose(1, 0, 2)
        .reshape(length)
    )
    query_order = query_start + jnp.arange(quarter, dtype=jnp.int32)
    allowed = (query_seg[:, :, None] == key_seg[:, None, :]) & (
        key_order[None, None, :] <= query_order[None, :, None]
    )
    x_in = inputs.astype(jnp.float32)
    normed_first, root_first = norm_apply(x_in, gain_first)
    first_tok = to_tokens(normed_first)
    query_lin = jnp.dot(first_tok, query_full, preferred_element_type=jnp.float32)
    key_lin = jnp.dot(first_tok, key_full, preferred_element_type=jnp.float32)
    value_own = jnp.dot(first_tok, value_full, preferred_element_type=jnp.float32).astype(
        jnp.bfloat16
    )
    cosine, sine_term = rotary(query_pos)
    query_rot = rotate(query_lin.reshape(seq_count, quarter, QH, HD), cosine, sine_term).astype(
        jnp.bfloat16
    )
    key_rot = rotate(key_lin.reshape(seq_count, quarter, KH, HD), cosine, sine_term).astype(
        jnp.bfloat16
    )
    kv_own = jnp.concatenate([key_rot.reshape(seq_count, quarter, KD), value_own], axis=2)
    kv_all = lax.all_gather(kv_own, ("row", "col"), axis=1, tiled=True)
    key_rows, value_rows = split_kv(kv_all, seq_count, length)
    query_grp = query_rot.reshape(seq_count, quarter, KH, QH // KH, HD)
    scores = masked_scores(query_grp, key_rows, allowed)
    row_max = jnp.max(scores, axis=-1, keepdims=True)
    weights_exp = jnp.exp(scores - row_max)
    row_sum = jnp.sum(weights_exp, axis=-1, keepdims=True)
    log_total = row_max + jnp.log(row_sum)
    attn_probs = (weights_exp / row_sum).astype(jnp.bfloat16)
    attended = jnp.einsum(
        "shgqk,skhd->sqhgd", attn_probs, value_rows, preferred_element_type=jnp.float32
    )
    attended = attended.reshape(seq_count, quarter, QD).astype(jnp.bfloat16)
    branch = jnp.dot(attended, output_full, preferred_element_type=jnp.float32).astype(jnp.bfloat16)
    middle = x_in + to_features(branch).astype(jnp.float32)
    normed_second, root_second = norm_apply(middle, gain_second)
    gate_full, up_full, down_full = (
        lax.all_gather(gate_weight, "row", axis=0, tiled=True),
        lax.all_gather(up_weight, "row", axis=0, tiled=True),
        lax.all_gather(down_weight, "row", axis=1, tiled=True),
    )
    second_tok = to_tokens(normed_second).reshape(own_rows, D)

    def project_in(piece_rows, first_row):
        gate_part = jnp.dot(piece_rows, gate_full, preferred_element_type=jnp.float32)
        up_part = jnp.dot(piece_rows, up_full, preferred_element_type=jnp.float32)
        return (gate_part, up_part, piece_rows)

    gate_lin, up_lin, second_rows = col_rows(second_tok, project_in)
    hidden = (jax.nn.silu(gate_lin) * up_lin).astype(jnp.bfloat16)

    def project_out(first_row, row_count):
        return jnp.dot(hidden, down_full, preferred_element_type=jnp.float32)

    ffn_out = col_sums(project_out, own_rows).astype(jnp.bfloat16).reshape(seq_count, quarter, D)
    layer_out = (middle + to_features(ffn_out).astype(jnp.float32)).astype(jnp.bfloat16)
    grad_out_tok = to_tokens(cotangent).reshape(own_rows, D)

    def hidden_back(piece_rows, first_row):
        grad_hidden = jnp.einsum(
            "td,fd->tf", piece_rows, down_full, preferred_element_type=jnp.float32
        )
        sigmoid_gate = jax.nn.sigmoid(gate_lin)
        grad_gate_part = (
            grad_hidden * up_lin * sigmoid_gate * (1.0 + gate_lin * (1.0 - sigmoid_gate))
        ).astype(jnp.bfloat16)
        grad_up_part = (grad_hidden * gate_lin * sigmoid_gate).astype(jnp.bfloat16)
        return (grad_gate_part, grad_up_part, piece_rows)

    grad_gate_lin, grad_up_lin, grad_out_rows = col_rows(grad_out_tok, hidden_back)
    down_part = jnp.einsum("tf,td->fd", hidden, grad_out_rows, preferred_element_type=jnp.float32)
    gate_part_grad = jnp.einsum(
        "td,tf->df", second_rows, grad_gate_lin, preferred_element_type=jnp.float32
    )
    up_part_grad = jnp.einsum(
        "td,tf->df", second_rows, grad_up_lin, preferred_element_type=jnp.float32
    )

    def input_back(first_row, row_count):
        return jnp.einsum(
            "tf,df->td", grad_gate_lin, gate_full, preferred_element_type=jnp.float32
        ) + jnp.einsum("tf,df->td", grad_up_lin, up_full, preferred_element_type=jnp.float32)

    grad_second = col_sums(input_back, own_rows).astype(jnp.bfloat16).reshape(seq_count, quarter, D)
    grad_second = to_features(grad_second).astype(jnp.float32)
    gate_blk, up_blk, down_blk = (
        lax.psum_scatter(
            gate_part_grad.astype(jnp.bfloat16), "row", scatter_dimension=0, tiled=True
        ).astype(jnp.float32),
        lax.psum_scatter(
            up_part_grad.astype(jnp.bfloat16), "row", scatter_dimension=0, tiled=True
        ).astype(jnp.float32),
        lax.psum_scatter(
            down_part.astype(jnp.bfloat16), "row", scatter_dimension=1, tiled=True
        ).astype(jnp.float32),
    )
    grad_mid_norm, gain_second_part = norm_back(middle, root_second, gain_second, grad_second)
    grad_middle = cotangent.astype(jnp.float32) + grad_mid_norm
    grad_branch = to_tokens(grad_middle.astype(jnp.bfloat16))
    output_part = jnp.einsum(
        "sqe,sqd->ed", attended, grad_branch, preferred_element_type=jnp.float32
    )
    grad_attended = jnp.einsum(
        "sqd,ed->sqe", grad_branch, output_full, preferred_element_type=jnp.float32
    ).astype(jnp.bfloat16)
    key_back, value_back = split_kv(kv_all, seq_count, length)
    exact_probs = jnp.exp(masked_scores(query_grp, key_back, allowed) - log_total)
    grad_att_grp = grad_attended.reshape(seq_count, quarter, KH, QH // KH, HD)
    grad_probs = jnp.einsum(
        "sqhgd,skhd->shgqk", grad_att_grp, value_back, preferred_element_type=jnp.float32
    )
    row_delta = jnp.sum(exact_probs * grad_probs, axis=-1, keepdims=True)
    grad_scores = (exact_probs * (grad_probs - row_delta)).astype(jnp.bfloat16)
    grad_query_rot = jnp.einsum(
        "shgqk,skhd->sqhgd", grad_scores, key_back, preferred_element_type=jnp.float32
    ) * HD ** (-0.5)
    grad_keys = jnp.einsum(
        "shgqk,sqhgd->skhd", grad_scores, query_grp, preferred_element_type=jnp.float32
    ) * HD ** (-0.5)
    grad_values = jnp.einsum(
        "shgqk,sqhgd->skhd",
        exact_probs.astype(jnp.bfloat16),
        grad_att_grp,
        preferred_element_type=jnp.float32,
    )
    grad_kv = jnp.concatenate(
        [grad_keys.reshape(seq_count, length, KD), grad_values.reshape(seq_count, length, KD)],
        axis=2,
    )
    grad_kv_own = lax.psum_scatter(
        grad_kv.astype(jnp.bfloat16), ("row", "col"), scatter_dimension=1, tiled=True
    ).astype(jnp.float32)
    grad_key_lin = (
        unrotate(grad_kv_own[..., :KD].reshape(seq_count, quarter, KH, HD), cosine, sine_term)
        .reshape(seq_count, quarter, KD)
        .astype(jnp.bfloat16)
    )
    grad_value_own = grad_kv_own[..., KD:].astype(jnp.bfloat16)
    grad_query_lin = (
        unrotate(grad_query_rot.reshape(seq_count, quarter, QH, HD), cosine, sine_term)
        .reshape(seq_count, quarter, QD)
        .astype(jnp.bfloat16)
    )
    query_part = jnp.einsum(
        "sqd,sqe->de", first_tok, grad_query_lin, preferred_element_type=jnp.float32
    )
    key_part = jnp.einsum(
        "sqd,sqe->de", first_tok, grad_key_lin, preferred_element_type=jnp.float32
    )
    value_part = jnp.einsum(
        "sqd,sqe->de", first_tok, grad_value_own, preferred_element_type=jnp.float32
    )
    grad_first_tok = jnp.einsum(
        "sqe,de->sqd", grad_query_lin, query_full, preferred_element_type=jnp.float32
    )
    grad_first_tok = grad_first_tok + jnp.einsum(
        "sqe,de->sqd", grad_key_lin, key_full, preferred_element_type=jnp.float32
    )
    grad_first_tok = grad_first_tok + jnp.einsum(
        "sqe,de->sqd", grad_value_own, value_full, preferred_element_type=jnp.float32
    )
    grad_first = to_features(grad_first_tok.astype(jnp.bfloat16)).astype(jnp.float32)
    grad_in_norm, gain_first_part = norm_back(x_in, root_first, gain_first, grad_first)
    input_grad = grad_middle + grad_in_norm
    gain_pair = jnp.stack([gain_first_part, gain_second_part], axis=1)
    block_rows = jnp.arange(row_size * col_size, dtype=jnp.int32) // col_size == row_index
    gain_spread = jnp.where(block_rows[:, None, None], gain_pair[None], 0.0).reshape(
        row_size * col_size * half_width, 2
    )
    query_blk, key_blk, value_blk, output_blk, gain_blk = (
        lax.psum_scatter(
            query_part.astype(jnp.bfloat16), ("row", "col"), scatter_dimension=0, tiled=True
        ).astype(jnp.float32),
        lax.psum_scatter(
            key_part.astype(jnp.bfloat16), ("row", "col"), scatter_dimension=0, tiled=True
        ).astype(jnp.float32),
        lax.psum_scatter(
            value_part.astype(jnp.bfloat16), ("row", "col"), scatter_dimension=0, tiled=True
        ).astype(jnp.float32),
        lax.psum_scatter(
            output_part.astype(jnp.bfloat16), ("row", "col"), scatter_dimension=0, tiled=True
        ).astype(jnp.float32),
        lax.psum_scatter(
            gain_spread.astype(jnp.bfloat16), ("row", "col"), scatter_dimension=0, tiled=True
        ).astype(jnp.float32),
    )
    query_sum, key_sum, value_sum, output_sum, gain_sum, gate_sum, up_sum, down_sum = lax.psum(
        (query_blk, key_blk, value_blk, output_blk, gain_blk, gate_blk, up_blk, down_blk), "dp"
    )
    return (
        layer_out,
        input_grad,
        gain_sum[:, 0],
        query_sum,
        key_sum,
        value_sum,
        output_sum,
        gain_sum[:, 1],
        gate_sum,
        up_sum,
        down_sum,
    )


def solution(mesh):
    placed = (
        P("dp", "col", "row"),
        P("dp", None),
        P("dp", None),
        P("row"),
        P(("row", "col"), None),
        P(("row", "col"), None),
        P(("row", "col"), None),
        P(("row", "col"), None),
        P("row"),
        P("row", "col"),
        P("row", "col"),
        P("col", "row"),
        P("dp", "col", "row"),
    )
    return jax.shard_map(
        local,
        mesh=mesh,
        in_specs=placed,
        out_specs=(
            P("dp", "col", "row"),
            P("dp", "col", "row"),
            P("row"),
            P(("row", "col"), None),
            P(("row", "col"), None),
            P(("row", "col"), None),
            P(("row", "col"), None),
            P("row"),
            P("row", "col"),
            P("row", "col"),
            P("col", "row"),
        ),
        check_vma=False,
    )
```

profile of v0, /device:TPU:0, one launch (start us, length us, event | category | flops | bytes accessed | tf_op | source)
XLA Modules:
  0.0 1312.1 jit_solution(5993376248561021840)
XLA Ops:
  24.9 35.1 %all-gather = bf16[4,240,320]{1,2,0:T(8,128)(2,1)} all-gather(bf16[1,240,320]{1,2,0:T(8,128)(2,1)S(1)} %bitcast.290), channel_id=1, replica_groups=mesh['dp'=8,'row'=2,'col'=2] {'row','col'}, dimensions={0}, use_global_device_ids=true | all-gather | bytes 768000 | tf_op jit(solution)/shard_map/all_gather | solution.py:122
  92.8 23.8 %all-gather.11.cloned.1.call-done = bf16[6,512,640]{1,2,0:T(8,128)(2,1)} async-done(((bf16[6,128,640]{1,2,0:T(8,128)(2,1)}), bf16[6,512,640]{1,2,0:T(8,128)(2,1)}) %all-gather.11.cloned.1.call-update) | async-done | bytes 3932176 | tf_op jit(solution)/shard_map/all_gather | solution.py:160
  129.2 10.5 fusion.3
  139.7 11.1 fusion.32
  156.3 43.2 %all_to_all.102 = bf16[6,128,960]{1,0,2:T(8,128)(2,1)S(1)} all-to-all(bf16[6,128,960]{1,0,2:T(8,128)(2,1)S(1)} %copy.109), channel_id=1, replica_groups=mesh['dp'=8,'row'=2,'col'=2] {'row'}, dimensions={2} | all-to-all | bytes 2949120 | tf_op jit(solution)/shard_map/all_to_all | solution.py:28
  218.1 27.7 %all_to_all.103 = bf16[6,256,480]{2,0,1:T(8,128)(2,1)S(1)} all-to-all(bf16[6,256,480]{2,0,1:T(8,128)(2,1)} %copy.111), channel_id=1, replica_groups=mesh['dp'=8,'row'=2,'col'=2] {'row'}, dimensions={1} | all-to-all | bytes 2949120 | tf_op jit(solution)/shard_map/all_to_all | solution.py:24
  258.4 37.3 %all_to_all.104 = bf16[6,256,480]{2,0,1:T(8,128)(2,1)S(1)} all-to-all(bf16[6,256,480]{2,0,1:T(8,128)(2,1)} %copy.117), channel_id=1, replica_groups=mesh['dp'=8,'row'=2,'col'=2] {'row'}, dimensions={1} | all-to-all | bytes 2949120 | tf_op jit(solution)/shard_map/all_to_all | solution.py:24
  323.2 27.4 %all-gather.23.cloned.1.call-done = bf16[1280,960]{0,1:T(8,128)(2,1)} async-done(((bf16[1280,480]{0,1:T(8,128)(2,1)}), bf16[1280,960]{0,1:T(8,128)(2,1)}) %all-gather.23.cloned.1.call-update) | async-done | bytes 2457616 | tf_op jit(solution)/shard_map/all_gather | solution.py:179
  350.6 14.3 %all-gather.25.cloned.1.call-done = bf16[1536,960]{1,0:T(8,128)(2,1)} async-done(((bf16[768,960]{1,0:T(8,128)(2,1)}), bf16[1536,960]{1,0:T(8,128)(2,1)}) %all-gather.25.cloned.1.call-update) | async-done | bytes 2949136 | tf_op jit(solution)/shard_map/all_gather | solution.py:32
  364.9 14.0 %multiply_convert_fusion = (bf16[1536,1280]{1,0:T(8,128)(2,1)S(1)}, bf16[1536,1280]{1,0:T(8,128)(2,1)S(1)}, bf16[1536,1280]{1,0:T(8,128)(2,1)}) fusion(f32[1536,1280]{1,0:T(8,128)} %fusion.55, f32[1536,1280]{1,0:T(8,128)} %fusion.56, bf16[1536,960]{1,0:T(8,128)(2,1)} %all-gather.25.cloned.1.call-done, bf16[1280,960]{0,1:T(8,128)(2,1)} %all-gather.23.cloned.1.call-done), kind=kOutput, calls=%fused_computation.15 | convolution fusion | flops 3806330880 | bytes 32931840 | tf_op jit(solution)/shard_map/td,fd->tf/dot_general | solution.py:199
  388.9 15.3 %reduce-scatter.22.cloned.1.call-done = f32[768,960]{0,1:T(8,128)} async-done(((f32[1536,960]{0,1:T(8,128)}), f32[768,960]{0,1:T(8,128)}) %reduce-scatter.22.cloned.1.call-update) | async-done | bytes 2949136 | tf_op jit(solution)/shard_map/reduce_scatter | solution.py:36
  413.8 27.9 %all_to_all.105 = bf16[6,128,960]{1,0,2:T(8,128)(2,1)S(1)} all-to-all(bf16[6,128,960]{1,0,2:T(8,128)(2,1)} %copy.120), channel_id=1, replica_groups=mesh['dp'=8,'row'=2,'col'=2] {'row'}, dimensions={2} | all-to-all | bytes 2949120 | tf_op jit(solution)/shard_map/all_to_all | solution.py:28
  462.9 23.6 %all-to-all-done.6 = bf16[6,256,480]{2,0,1:T(8,128)(2,1)} async-done(((bf16[6,256,480]{2,0,1:T(8,128)(2,1)}), bf16[6,256,480]{2,0,1:T(8,128)(2,1)}, u32[]{:S(2)}, u32[]{:S(2)}) %all-to-all-start.6) | async-done | bytes 1474592 | tf_op jit(solution)/shard_map/all_to_all | solution.py:24
  495.9 11.5 bitcast_convert_fusion.2
  507.4 16.3 %fusion = (f32[6,5,3,128]{3,2,1,0:T(4,128)S(1)}, f32[6,5,512,128,3]{3,2,4,1,0:T(8,128)}) fusion(f32[6,5,3,128]{3,2,1,0:T(4,128)S(1)} %log_add_fusion, f32[6,5,512,128,3]{3,2,4,1,0:T(8,128)} %get-tuple-element.51, pred[6,128,512]{1,2,0:T(8,128)(4,1)S(1)} %compare_and_fusion, bf16[6,512,5,64,1]{1,3,4,2,0:T(8,128)(2,1)} %bitcast.252, ...), kind=kOutput, calls=%fused_computation.2 | convolution fusion | flops 784454400 | bytes 51111936 | tf_op jit(solution)/shard_map/sqhgd,skhd->shgqk/dot_general | solution.py:248
  523.8 20.4 %fusion.2 = bf16[6,5,3,128,512]{3,4,2,1,0:T(8,128)(2,1)} fusion(f32[6,5,512,128,3]{3,2,4,1,0:T(8,128)} %get-tuple-element.53, f32[6,5,3,128]{3,2,1,0:T(4,128)S(1)} %get-tuple-element.52, f32[6,5,3,128]{3,2,1,0:T(4,128)S(1)} %log_add_fusion, f32[6,5,512,128,3]{3,2,4,1,0:T(8,128)} %get-tuple-element.51, pred[6,128,512]{1,2,0:T(8,128)(4,1)S(1)} %compare_and_fusion), kind=kLoop, calls=%fused_computation.4 | loop fusion | flops 35389440 | bytes 59467776 | tf_op jit(solution)/shard_map/convert_element_type | solution.py:252
  653.1 34.4 %all-to-all-done.7 = bf16[6,128,960]{1,0,2:T(8,128)(2,1)} async-done(((bf16[6,128,960]{1,0,2:T(8,128)(2,1)}), bf16[6,128,960]{1,0,2:T(8,128)(2,1)}, u32[]{:S(2)}, u32[]{:S(2)}) %all-to-all-start.7) | async-done | bytes 1474592 | tf_op jit(solution)/shard_map/all_to_all | solution.py:28
  727.7 45.5 %reduce-scatter.30.cloned.1.call-done = bf16[480,1280]{1,0:T(8,128)(2,1)} async-done(((bf16[960,1280]{1,0:T(8,128)(2,1)}), bf16[480,1280]{1,0:T(8,128)(2,1)}) %reduce-scatter.30.cloned.1.call-update) | async-done | bytes 1228816 | tf_op jit(solution)/shard_map/reduce_scatter | solution.py:229
  776.0 30.3 %reduce-scatter.26.cloned.1.call-done = bf16[240,960]{1,0:T(8,128)(2,1)} async-done(((bf16[960,960]{1,0:T(8,128)(2,1)}), bf16[240,960]{1,0:T(8,128)(2,1)}) %reduce-scatter.26.cloned.1.call-update) | async-done | bytes 460816 | tf_op jit(solution)/shard_map/reduce_scatter | solution.py:319
  806.3 33.1 %reduce-scatter.24.cloned.1.call-done = bf16[240,960]{1,0:T(8,128)(2,1)} async-done(((bf16[960,960]{1,0:T(8,128)(2,1)}), bf16[240,960]{1,0:T(8,128)(2,1)}) %reduce-scatter.24.cloned.1.call-update) | async-done | bytes 460816 | tf_op jit(solution)/shard_map/reduce_scatter | solution.py:310
  850.5 12.9 reduce-scatter.36.cloned.1.call-done
  864.4 25.1 %reduce-scatter.40.cloned.1.call-done = bf16[240,320]{1,0:T(8,128)(2,1)} async-done(((bf16[960,320]{1,0:T(8,128)(2,1)}), bf16[240,320]{1,0:T(8,128)(2,1)}) %reduce-scatter.40.cloned.1.call-update) | async-done | bytes 153616
  890.5 25.1 %reduce-scatter.38.cloned.1.call-done = bf16[240,320]{1,0:T(8,128)(2,1)} async-done(((bf16[960,320]{1,0:T(8,128)(2,1)}), bf16[240,320]{1,0:T(8,128)(2,1)}) %reduce-scatter.38.cloned.1.call-update) | async-done | bytes 153616
  916.6 388.2 %all-reduce.2 = (f32[480,2]{0,1:T(2,128)S(1)}, f32[240,960]{1,0:T(8,128)}, f32[240,320]{0,1:T(8,128)}, f32[240,320]{0,1:T(8,128)}, f32[240,960]{1,0:T(8,128)}, /...) all-reduce(bf16[480,2]{0,1:T(2,128)(2,1)S(1)} %copy.144, ...), channel_id=1, replica_groups=mesh['dp'=8,'row'=2,'col'=2] {'dp'}, use_global_device_ids=true, to_apply=%region_17.18 | all-reduce | flops 2458560 | bytes 14751360 | tf_op jit(solution)/shard_map/psum | solution.py:326
  (244 shorter events, 343.2 us)
Async XLA Ops:
  7.2 78.2 %all-gather.13.cloned.1.call-start = ((), (), s32[]{:S(2)}) async-start(), calls=%async_computation.20 | async-start | bytes 2457600 | tf_op jit(solution)/shard_map/all_gather | solution.py:121
  20.9 55.1 %all-to-all-start = ((bf16[6,256,480]{2,0,1:T(8,128)(2,1)}), bf16[6,256,480]{2,0,1:T(8,128)(2,1)S(1)}, u32[]{:S(2)}, u32[]{:S(2)}) async-start(bf16[6,256,480]{2,0,1:T(8,128)(2,1)} %copy.101), calls=%async_computation | async-start | bytes 4194304 | tf_op jit(solution)/shard_map/all_to_all | solution.py:24
  24.8 91.8 %all-gather.11.cloned.1.call-start = ((), (), s32[]{:S(2)}) async-start(), calls=%async_computation.19 | async-start | bytes 4915200 | tf_op jit(solution)/shard_map/all_gather | solution.py:160
  83.0 68.0 %all-gather.15.cloned.1.call-start = ((), (), s32[]{:S(2)}) async-start(), calls=%async_computation.21 | async-start | bytes 2457600 | tf_op jit(solution)/shard_map/all_gather | solution.py:124
  83.7 219.2 %all-gather.21.cloned.1.call-start = ((), (), s32[]{:S(2)}) async-start(), calls=%async_computation.24 | async-start | bytes 3686400 | tf_op jit(solution)/shard_map/all_gather | solution.py:178
  84.3 218.7 %all-gather.17.cloned.1.call-start = ((), (), s32[]{:S(2)}) async-start(), calls=%async_computation.22 | async-start | bytes 4718592 | tf_op jit(solution)/shard_map/all_gather | solution.py:32
  252.6 60.3 %all-gather.19.cloned.1.call-start = ((), (), s32[]{:S(2)}) async-start(), calls=%async_computation.23 | async-start | bytes 3686400 | tf_op jit(solution)/shard_map/all_gather | solution.py:177
  253.2 97.4 %all-gather.23.cloned.1.call-start = ((), (), s32[]{:S(2)}) async-start(), calls=%async_computation.25 | async-start | bytes 3686400 | tf_op jit(solution)/shard_map/all_gather | solution.py:179
  253.9 111.0 %all-gather.25.cloned.1.call-start = ((), (), s32[]{:S(2)}) async-start(), calls=%async_computation.27 | async-start | bytes 4718592 | tf_op jit(solution)/shard_map/all_gather | solution.py:32
  302.4 101.7 %reduce-scatter.22.cloned.1.call-start = ((), (), s32[]{:S(2)}) async-start(), calls=%async_computation.28 | async-start | bytes 8847360 | tf_op jit(solution)/shard_map/reduce_scatter | solution.py:36
  457.9 28.6 %all-to-all-start.6 = ((bf16[6,256,480]{2,0,1:T(8,128)(2,1)}), bf16[6,256,480]{2,0,1:T(8,128)(2,1)}, u32[]{:S(2)}, u32[]{:S(2)}) async-start(bf16[6,256,480]{2,0,1:T(8,128)(2,1)} %copy.123), calls=%async_computation.8 | async-start | bytes 4194304 | tf_op jit(solution)/shard_map/all_to_all | solution.py:24
  462.8 167.6 %reduce-scatter.34.cloned.1.call-start = ((), (), s32[]{:S(2)}) async-start(), calls=%async_computation.34 | async-start | bytes 4915200
  568.4 139.4 %reduce-scatter.20.cloned.1.call-start = ((), (), s32[]{:S(2)}) async-start(), calls=%async_computation.26 | async-start | bytes 8847360 | tf_op jit(solution)/shard_map/reduce_scatter | solution.py:36
  578.6 149.0 %reduce-scatter.32.cloned.1.call-start = ((), (), s32[]{:S(2)}) async-start(), calls=%async_computation.33 | async-start | bytes 3686400 | tf_op jit(solution)/shard_map/reduce_scatter | solution.py:232
  587.4 140.2 %reduce-scatter.28.cloned.1.call-start = ((), (), s32[]{:S(2)}) async-start(), calls=%async_computation.31 | async-start | bytes 3686400 | tf_op jit(solution)/shard_map/reduce_scatter | solution.py:226
  596.2 177.0 %reduce-scatter.30.cloned.1.call-start = ((), (), s32[]{:S(2)}) async-start(), calls=%async_computation.32 | async-start | bytes 3686400 | tf_op jit(solution)/shard_map/reduce_scatter | solution.py:229
  604.8 201.4 %reduce-scatter.26.cloned.1.call-start = ((), (), s32[]{:S(2)}) async-start(), calls=%async_computation.30 | async-start | bytes 2457600 | tf_op jit(solution)/shard_map/reduce_scatter | solution.py:319
  609.8 229.5 %reduce-scatter.24.cloned.1.call-start = ((), (), s32[]{:S(2)}) async-start(), calls=%async_computation.29 | async-start | bytes 2457600 | tf_op jit(solution)/shard_map/reduce_scatter | solution.py:310
  647.9 39.6 %all-to-all-start.7 = ((bf16[6,128,960]{1,0,2:T(8,128)(2,1)}), bf16[6,128,960]{1,0,2:T(8,128)(2,1)}, u32[]{:S(2)}, u32[]{:S(2)}) async-start(bf16[6,128,960]{1,0,2:T(8,128)(2,1)} %copy.128), calls=%async_computation.9 | async-start | bytes 3932160 | tf_op jit(solution)/shard_map/all_to_all | solution.py:28
  652.7 210.7 %reduce-scatter.36.cloned.1.call-start = ((), (), s32[]{:S(2)}) async-start(), calls=%async_computation.35 | async-start | bytes 614400
  702.5 186.9 %reduce-scatter.40.cloned.1.call-start = ((), (), s32[]{:S(2)}) async-start(), calls=%async_computation.37 | async-start | bytes 921600
  717.6 55.6 %all-to-all-start.3 = ((bf16[6,128,960]{1,0,2:T(8,128)(2,1)}), bf16[6,128,960]{1,0,2:T(8,128)(2,1)}, u32[]{:S(2)}, u32[]{:S(2)}) async-start(bf16[6,128,960]{1,0,2:T(8,128)(2,1)} %copy.114), calls=%async_computation.4 | async-start | bytes 3932160 | tf_op jit(solution)/shard_map/all_to_all | solution.py:28
  722.3 193.2 %reduce-scatter.38.cloned.1.call-start = ((), (), s32[]{:S(2)}) async-start(), calls=%async_computation.36 | async-start | bytes 921600
  725.3 119.0 %copy-start.30 = (f32[6,256]{1,0:T(8,128)S(1)}, f32[6,256]{1,0:T(8,128)}, u32[]{:S(2)}) copy-start(f32[6,256]{1,0:T(8,128)} %get-tuple-element.42) | copy-start | bytes 18436
  (39 other events, 380.3 us)
Sparse Core Ops, SparseCore 0:
  9.6 30.1 all-gather.12
  83.1 33.5 all-gather.10
  118.2 21.8 all-gather.14
  141.5 53.5 all-gather.20
  252.7 12.1 all-gather.16
  266.3 45.5 all-gather.18
  313.4 37.1 all-gather.22
  352.7 12.1 all-gather.24
  389.0 15.1 reduce-scatter.21
  568.5 43.0 reduce-scatter.33
  614.0 13.9 reduce-scatter.19
  630.8 48.2 reduce-scatter.31
  682.0 35.9 reduce-scatter.27
  720.8 52.2 reduce-scatter.29
  775.7 30.4 reduce-scatter.25
  808.7 30.6 reduce-scatter.23
  841.9 21.4 reduce-scatter.35
  866.5 22.9 reduce-scatter.39
  892.6 22.9 reduce-scatter.37
where the time goes:
time: 1320 us; the launch traced here: 1310 us
  blocking collectives  588 us (45%)
  waiting for transfers between devices  314 us (24%)
  matrix products  179 us (14%)
  local copies, waits for them, and re-layouts  127 us (10%)
  other arithmetic  68.3 us (5%)
  starting transfers between devices  20.2 us (2%)
  between operations  15 us (1%)
    psum x1, blocking collectives, local(): lax.psum((query_blk, key_blk, value_blk, output_blk, gain_blk, gate_blk,...  388 us
    all_to_all x2, blocking collectives, to_features(): lax.all_to_all(values, 'row', split_axis=2, concat_axis=1, tiled=True)  71.1 us
    unnamed x23, waiting for transfers between devices  66.4 us
    all_to_all x2, blocking collectives, to_tokens(): lax.all_to_all(values, 'row', split_axis=1, concat_axis=2, tiled=True)  65 us
    unnamed x95, local copies, waits for them, and re-layouts  47.4 us
    reduce_scatter x1, waiting for transfers between devices, local(): lax.psum_scatter(up_part_grad.astype(jnp.bfloat16), 'row', scatter_dimens...  45.5 us
    all_gather x1, blocking collectives, local(): lax.all_gather(key_weight, ('row', 'col'), axis=0, tiled=True)  35.1 us
    all_to_all x2, waiting for transfers between devices, to_features(): lax.all_to_all(values, 'row', split_axis=2, concat_axis=1, tiled=True)  34.4 us
  transfers between devices with their start and end apart: 23, of which 12 were waited for; matrix products, arithmetic and copies ran while one was open for 18% of the time, Pallas kernels for 0%

commit v1 on v0

v1 whole, which is shorter than its diff:
```python
import jax
import jax.numpy as jnp
from jax import lax
from jax.sharding import PartitionSpec as P

D = 960
QH = 15
KH = 5
HD = 64
QD = 960
KD = 320


eps_norm = 1e-05
rope_base = 10000.0
masked_value = -1e30


def swap(values, axis_name):
    size = lax.axis_size(axis_name)
    return lax.ppermute(values, axis_name, [(i, size - 1 - i) for i in range(size)])


def ordered(own, other, index, axis):
    return jnp.where(
        index == 0,
        jnp.concatenate([own, other], axis=axis),
        jnp.concatenate([other, own], axis=axis),
    )


def half_of(values, index, axis):
    size = values.shape[axis] // 2
    return lax.dynamic_slice_in_dim(values, index * size, size, axis)


def to_tokens(values, row_index):
    other = swap(half_of(values, 1 - row_index, 1), "row")
    return ordered(half_of(values, row_index, 1), other, row_index, 2)


def to_features(values, row_index):
    other = swap(half_of(values, 1 - row_index, 2), "row")
    return ordered(half_of(values, row_index, 2), other, row_index, 1)


def gather_rows(own, row_index, col_index):
    pair = ordered(own[None], swap(own, "row")[None], row_index, 0)
    full = ordered(pair[:, None], swap(pair, "col")[:, None], col_index, 1)
    return full.reshape(-1, own.shape[1])


def scatter_rows(part, row_index, col_index):
    blocks = part.reshape(2, 2, part.shape[0] // 4, part.shape[1])
    keep = half_of(blocks, col_index, 1)[:, 0]
    away = half_of(blocks, 1 - col_index, 1)[:, 0]
    pair = keep + swap(away.astype(jnp.bfloat16), "col").astype(jnp.float32)
    own = half_of(pair, row_index, 0)[0]
    send = half_of(pair, 1 - row_index, 0)[0]
    return own + swap(send.astype(jnp.bfloat16), "row").astype(jnp.float32)


def dp_total(values, dim):
    part = lax.psum_scatter(
        values.astype(jnp.bfloat16), "dp", scatter_dimension=dim, tiled=True
    )
    return lax.all_gather(part, "dp", axis=dim, tiled=True)


def norm_apply(values, gain):
    inv_root = lax.rsqrt(jnp.mean(values * values, axis=-1, keepdims=True) + eps_norm)
    return ((values * inv_root * gain).astype(jnp.bfloat16), inv_root)


def norm_back(values, inv_root, gain, grad_normed):
    weighted = grad_normed * gain
    cross = jnp.sum(weighted * values, axis=-1, keepdims=True)
    grad_values = inv_root * weighted - values * inv_root**3 * cross / D
    gain_part = jnp.sum(grad_normed * values * inv_root, axis=(0, 1))
    return (grad_values, gain_part)


def dot(spec, left, right):
    return jnp.einsum(spec, left, right, preferred_element_type=jnp.float32)


def rotary(pos_rows):
    frequency = rope_base ** (-(jnp.arange(HD // 2, dtype=jnp.float32) * 2.0 / HD))
    angle_grid = pos_rows.astype(jnp.float32)[..., None] * frequency
    return (jnp.cos(angle_grid)[:, :, None, :], jnp.sin(angle_grid)[:, :, None, :])


def rotate(values, cosine, sine_term):
    half_dim = values.shape[-1] // 2
    lead_half = values[..., :half_dim]
    tail_half = values[..., half_dim:]
    return jnp.concatenate(
        [lead_half * cosine - tail_half * sine_term, tail_half * cosine + lead_half * sine_term],
        axis=-1,
    )


def unrotate(grads, cosine, sine_term):
    half_dim = grads.shape[-1] // 2
    lead_half = grads[..., :half_dim]
    tail_half = grads[..., half_dim:]
    return jnp.concatenate(
        [lead_half * cosine + tail_half * sine_term, tail_half * cosine - lead_half * sine_term],
        axis=-1,
    )


def masked_scores(query_grp, key_rows, allowed):
    scores = jnp.einsum(
        "sqhgd,skhd->shgqk", query_grp, key_rows, preferred_element_type=jnp.float32
    ) * HD ** (-0.5)
    return jnp.where(allowed[:, None, None], scores, masked_value)


def split_kv(kv_rows, seq_count, length):
    key_rows = kv_rows[..., :KD].reshape(seq_count, length, KH, HD)
    value_rows = kv_rows[..., KD:].reshape(seq_count, length, KH, HD)
    return (key_rows, value_rows)


def local(
    inputs,
    segments,
    positions,
    gain_first,
    query_weight,
    key_weight,
    value_weight,
    output_weight,
    gain_second,
    gate_weight,
    up_weight,
    down_weight,
    cotangent,
):
    seq_count, half_len, half_width = inputs.shape
    length = segments.shape[1]
    quarter = length // 4
    own_rows = seq_count * quarter
    dp_size = lax.axis_size("dp")
    dp_index = lax.axis_index("dp")
    row_index = lax.axis_index("row")
    col_index = lax.axis_index("col")
    bf16 = jnp.bfloat16

    x_tok = to_tokens(inputs, row_index).astype(jnp.float32)
    qkv_full = gather_rows(
        jnp.concatenate([query_weight, key_weight, value_weight], axis=1), row_index, col_index
    )

    own_ffn = jnp.stack([gate_weight.T, up_weight.T, down_weight])
    units = own_ffn.shape[1]
    piece = units // dp_size
    ffn_slice = jnp.stack(
        [
            lax.dynamic_slice_in_dim(gate_weight, dp_index * piece, piece, 1).T,
            lax.dynamic_slice_in_dim(up_weight, dp_index * piece, piece, 1).T,
            lax.dynamic_slice_in_dim(down_weight, dp_index * piece, piece, 0),
        ]
    )
    other_ffn = lax.all_gather(swap(ffn_slice, "row"), "dp", axis=1, tiled=True)
    ffn_full = ordered(own_ffn, other_ffn, row_index, 2)
    gate_full, up_full, down_full = ffn_full[0], ffn_full[1], ffn_full[2]
    output_full = gather_rows(output_weight, row_index, col_index)
    gain_own = jnp.stack([gain_first, gain_second])
    gain_full = ordered(gain_own, swap(gain_own, "row"), row_index, 1)
    dy_own = to_tokens(cotangent, row_index)

    starts = [
        (c * 2 + r) * quarter
        for c, r in (
            (col_index, row_index),
            (col_index, 1 - row_index),
            (1 - col_index, row_index),
            (1 - col_index, 1 - row_index),
        )
    ]
    span = jnp.arange(quarter, dtype=jnp.int32)
    query_pos = lax.dynamic_slice_in_dim(positions, starts[0], quarter, 1)
    query_seg = lax.dynamic_slice_in_dim(segments, starts[0], quarter, 1)
    key_seg = jnp.concatenate(
        [lax.dynamic_slice_in_dim(segments, s, quarter, 1) for s in starts], axis=1
    )
    key_order = jnp.concatenate([s + span for s in starts])
    query_order = starts[0] + span
    allowed = (query_seg[:, :, None] == key_seg[:, None, :]) & (
        key_order[None, None, :] <= query_order[None, :, None]
    )

    first_tok, root_first = norm_apply(x_tok, gain_full[0])
    qkv_lin = dot("sqd,de->sqe", first_tok, qkv_full)
    cosine, sine_term = rotary(query_pos)
    key_rot = rotate(
        qkv_lin[..., QD : QD + KD].reshape(seq_count, quarter, KH, HD), cosine, sine_term
    ).astype(bf16)
    kv_own = jnp.concatenate(
        [key_rot.reshape(seq_count, quarter, KD), qkv_lin[..., QD + KD :].astype(bf16)], axis=2
    )
    kv_pair = jnp.concatenate([kv_own, swap(kv_own, "row")], axis=1)
    kv_all = jnp.concatenate([kv_pair, swap(kv_pair, "col")], axis=1)
    query_rot = rotate(
        qkv_lin[..., :QD].reshape(seq_count, quarter, QH, HD), cosine, sine_term
    ).astype(bf16)
    key_rows, value_rows = split_kv(kv_all, seq_count, length)
    query_grp = query_rot.reshape(seq_count, quarter, KH, QH // KH, HD)
    scores = masked_scores(query_grp, key_rows, allowed)
    row_max = jnp.max(scores, axis=-1, keepdims=True)
    weights_exp = jnp.exp(scores - row_max)
    row_sum = jnp.sum(weights_exp, axis=-1, keepdims=True)
    log_total = row_max + jnp.log(row_sum)
    attn_probs = (weights_exp / row_sum).astype(bf16)
    attended = dot("shgqk,skhd->sqhgd", attn_probs, value_rows)
    attended = attended.reshape(seq_count, quarter, QD).astype(bf16)
    branch = dot("sqe,ed->sqd", attended, output_full).astype(bf16)
    middle = x_tok + branch.astype(jnp.float32)
    normed_second, root_second = norm_apply(middle, gain_full[1])

    second = normed_second.reshape(own_rows, D)
    dy_rows = dy_own.reshape(own_rows, D)
    rows = [second, swap(second, "col")]
    dys = [dy_rows, swap(dy_rows, "col")]
    gates = [dot("td,fd->tf", v, gate_full) for v in rows]
    ups = [dot("td,fd->tf", v, up_full) for v in rows]
    hiddens = [(jax.nn.silu(g) * u).astype(bf16) for g, u in zip(gates, ups)]

    def back(dy, gate_lin, up_lin):
        grad_hidden = dot("td,fd->tf", dy, down_full)
        sig = jax.nn.sigmoid(gate_lin)
        grad_gate = (grad_hidden * up_lin * sig * (1.0 + gate_lin * (1.0 - sig))).astype(bf16)
        return (grad_gate, (grad_hidden * gate_lin * sig).astype(bf16))

    backs = [back(*v) for v in zip(dys, gates, ups)]

    def input_back(pair):
        return dot("tf,fd->td", pair[0], gate_full) + dot("tf,fd->td", pair[1], up_full)

    second_away = swap(input_back(backs[1]).astype(bf16), "col").astype(jnp.float32)
    grad_second = (input_back(backs[0]) + second_away).astype(bf16)
    grad_second = grad_second.reshape(seq_count, quarter, D).astype(jnp.float32)
    out_away = swap(dot("tf,fd->td", hiddens[1], down_full).astype(bf16), "col")
    ffn_out = (dot("tf,fd->td", hiddens[0], down_full) + out_away.astype(jnp.float32)).astype(bf16)
    layer_tok = (
        middle + ffn_out.reshape(seq_count, quarter, D).astype(jnp.float32)
    ).astype(bf16)
    layer_out = to_features(layer_tok, row_index)

    def weight_part(side):
        row_cut = [half_of(v, side, 1) for v in rows]
        dy_cut = [half_of(v, side, 1) for v in dys]

        def one(tall, wide):
            return dot("tf,td->fd", tall[0], wide[0]) + dot("tf,td->fd", tall[1], wide[1])

        return [
            one([b[0] for b in backs], row_cut),
            one([b[1] for b in backs], row_cut),
            one(hiddens, dy_cut),
        ]

    away = [v.astype(bf16) for v in weight_part(1 - row_index)]
    arrived = [swap(v, "row") for v in away]
    kept = weight_part(row_index)

    grad_mid_norm, gain_second_part = norm_back(middle, root_second, gain_full[1], grad_second)
    grad_middle = dy_own.astype(jnp.float32) + grad_mid_norm
    grad_branch = grad_middle.astype(bf16)
    grad_branch, away, kept = lax.optimization_barrier((grad_branch, away, kept))
    ffn_part = jnp.concatenate(
        [(k + a.astype(jnp.float32)).astype(bf16) for k, a in zip(kept, arrived)], axis=0
    )
    output_part = dot("sqe,sqd->ed", attended, grad_branch)
    grad_attended = dot("sqd,ed->sqe", grad_branch, output_full).astype(bf16)
    exact_probs = jnp.exp(masked_scores(query_grp, key_rows, allowed) - log_total)
    grad_att_grp = grad_attended.reshape(seq_count, quarter, KH, QH // KH, HD)
    grad_probs = dot("sqhgd,skhd->shgqk", grad_att_grp, value_rows)
    row_delta = jnp.sum(exact_probs * grad_probs, axis=-1, keepdims=True)
    grad_scores = (exact_probs * (grad_probs - row_delta)).astype(bf16)
    grad_keys = dot("shgqk,sqhgd->skhd", grad_scores, query_grp) * HD ** (-0.5)
    grad_values = dot("shgqk,sqhgd->skhd", exact_probs.astype(bf16), grad_att_grp)
    grad_kv = jnp.concatenate(
        [grad_keys.reshape(seq_count, length, KD), grad_values.reshape(seq_count, length, KD)],
        axis=2,
    ).astype(bf16)
    near = 2 * quarter
    kv_sum = grad_kv[:, :near].astype(jnp.float32) + swap(grad_kv[:, near:], "col").astype(
        jnp.float32
    )
    grad_kv_own = kv_sum[:, :quarter] + swap(kv_sum[:, quarter:].astype(bf16), "row").astype(
        jnp.float32
    )
    grad_query_rot = dot("shgqk,skhd->sqhgd", grad_scores, key_rows) * HD ** (-0.5)
    grad_query_lin = (
        unrotate(grad_query_rot.reshape(seq_count, quarter, QH, HD), cosine, sine_term)
        .reshape(seq_count, quarter, QD)
        .astype(bf16)
    )
    grad_key_lin = (
        unrotate(grad_kv_own[..., :KD].reshape(seq_count, quarter, KH, HD), cosine, sine_term)
        .reshape(seq_count, quarter, KD)
        .astype(bf16)
    )
    grad_kv_lin = jnp.concatenate([grad_key_lin, grad_kv_own[..., KD:].astype(bf16)], axis=2)
    query_part = dot("sqd,sqe->de", first_tok, grad_query_lin)
    kv_part = dot("sqd,sqe->de", first_tok, grad_kv_lin)
    grad_first = dot("sqe,de->sqd", grad_query_lin, qkv_full[:, :QD]) + dot(
        "sqe,de->sqd", grad_kv_lin, qkv_full[:, QD:]
    )
    grad_first = grad_first.astype(bf16).astype(jnp.float32)
    grad_in_norm, gain_first_part = norm_back(x_tok, root_first, gain_full[0], grad_first)
    input_grad = to_features((grad_middle + grad_in_norm).astype(bf16), row_index).astype(
        jnp.float32
    )

    ffn_sum = dp_total(ffn_part, 0).astype(jnp.float32)
    qo_part = jnp.concatenate([query_part, output_part], axis=1)
    qo_sum = dp_total(scatter_rows(qo_part, row_index, col_index), 1).astype(jnp.float32)
    kv_grad = dp_total(scatter_rows(kv_part, row_index, col_index), 1).astype(jnp.float32)
    gain_sum = lax.psum(jnp.stack([gain_first_part, gain_second_part]), ("dp", "row", "col"))
    gain_sum = half_of(gain_sum, row_index, 1)
    return (
        layer_out,
        input_grad,
        gain_sum[0],
        qo_sum[:, :QD],
        kv_grad[:, :KD],
        kv_grad[:, KD:],
        qo_sum[:, QD:],
        gain_sum[1],
        ffn_sum[:units].T,
        ffn_sum[units : 2 * units].T,
        ffn_sum[2 * units :],
    )


def solution(mesh):
    placed = (
        P("dp", "col", "row"),
        P("dp", None),
        P("dp", None),
        P("row"),
        P(("row", "col"), None),
        P(("row", "col"), None),
        P(("row", "col"), None),
        P(("row", "col"), None),
        P("row"),
        P("row", "col"),
        P("row", "col"),
        P("col", "row"),
        P("dp", "col", "row"),
    )
    return jax.shard_map(
        local,
        mesh=mesh,
        in_specs=placed,
        out_specs=(
            P("dp", "col", "row"),
            P("dp", "col", "row"),
            P("row"),
            P(("row", "col"), None),
            P(("row", "col"), None),
            P(("row", "col"), None),
            P(("row", "col"), None),
            P("row"),
            P("row", "col"),
            P("row", "col"),
            P("col", "row"),
        ),
        check_vma=False,
    )
```

time: 1320 us -> 727 us (0.55)
  blocking collectives: 588 us -> 130 us
  waiting for transfers between devices: 314 us -> 163 us
  other arithmetic: 68.3 us -> 117 us
  local copies, waits for them, and re-layouts: 127 us -> 91.2 us
    psum x5 -> x1, blocking collectives: 409 us -> 63.2 us  [local(): lax.psum(jnp.stack([gain_first_part, gain_second_part]), ('dp', 'row', 'c...]
    all_to_all x4 -> x0, blocking collectives: 136 us -> none  [the longest x2 71.1 us: to_features(): lax.all_to_all(values, 'row', split_axis=2, concat_axis=1, tiled=True)]
    ppermute x0 -> x25, waiting for transfers between devices: none -> 131 us  [swap(): lax.ppermute(values, axis_name, [(i, size - 1 - i) for i in range(size)])]
    reduce_scatter x7 -> x1, waiting for transfers between devices: 124 us -> 0.02 us  [dp_total(): lax.psum_scatter(values.astype(jnp.bfloat16), 'dp', scatter_dimension=dim...]
    unnamed x23 -> x7, waiting for transfers between devices: 66.4 us -> 0.09 us
    all_to_all x4 -> x0, waiting for transfers between devices: 58 us -> none  [the longest x2 34.4 us: to_features(): lax.all_to_all(values, 'row', split_axis=2, concat_axis=1, tiled=True)]
    all_gather x8 -> x2, waiting for transfers between devices: 65.6 us -> 31.8 us  [the longest x1 31.8 us: dp_total(): return lax.all_gather(part, 'dp', axis=dim, tiled=True)]
    select_n x0 -> x10, other arithmetic: none -> 30.6 us  [ordered(): jnp.where(index == 0, jnp.concatenate([own, other], axis=axis), jnp.conca...]
  transfers between devices with their start and end apart: 23 -> 30, of which waited for: 12 -> 11; matrix products, arithmetic and copies ran while one was open for 18% -> 44% of each run, Pallas kernels for 0% -> 0%
where the time goes in v1:
time: 727 us; the launch traced here: 717 us
  matrix products  178 us (24%)
  waiting for transfers between devices  163 us (22%)
  blocking collectives  130 us (18%)
  other arithmetic  117 us (16%)
  local copies, waits for them, and re-layouts  91.2 us (13%)
  starting transfers between devices  23.8 us (3%)
  between operations  15.4 us (2%)
    dot_general x37, matrix products, dot(): return jnp.einsum(spec, left, right, preferred_element_type=jnp.float32)  168 us
    ppermute x25, waiting for transfers between devices, swap(): lax.ppermute(values, axis_name, [(i, size - 1 - i) for i in range(size)])  131 us
    all_gather x2, blocking collectives, dp_total(): return lax.all_gather(part, 'dp', axis=dim, tiled=True)  66.9 us
    psum x1, blocking collectives, local(): lax.psum(jnp.stack([gain_first_part, gain_second_part]), ('dp', 'row', 'c...  63.2 us
    unnamed x155, local copies, waits for them, and re-layouts  38.8 us
    all_gather x1, waiting for transfers between devices, dp_total(): return lax.all_gather(part, 'dp', axis=dim, tiled=True)  31.8 us
    select_n x10, other arithmetic, ordered(): jnp.where(index == 0, jnp.concatenate([own, other], axis=axis), jnp.conca...  30.6 us
    ppermute x25, starting transfers between devices, swap(): lax.ppermute(values, axis_name, [(i, size - 1 - i) for i in range(size)])  23.5 us
  transfers between devices with their start and end apart: 30, of which 11 were waited for; matrix products, arithmetic and copies ran while one was open for 44% of the time, Pallas kernels for 0%

profile of v1, /device:TPU:0, one launch (start us, length us, event | category | flops | bytes accessed | tf_op | source)
XLA Modules:
  0.0 717.2 jit_solution(10382802638624087925)
XLA Ops:
  14.4 17.1 %collective-permute-done.2 = bf16[240,1600]{1,0:T(8,128)(2,1)S(1)} collective-permute-done((bf16[240,1600]{1,0:T(8,128)(2,1)S(1)}, bf16[240,1600]{1,0:T(8,128)(2,1)S(1)}, u32[]{:S(2)}, u32[]{:S(2)}) %collective-permute-start.2) | collective-permute-done | bytes 768032 | tf_op jit(solution)/shard_map/ppermute | solution.py:21
  38.4 16.0 %collective-permute-done = bf16[6,128,480]{1,2,0:T(8,128)(2,1)S(1)} collective-permute-done((bf16[6,128,480]{1,2,0:T(8,128)(2,1)}, bf16[6,128,480]{1,2,0:T(8,128)(2,1)S(1)}, u32[]{:S(2)}, u32[]{:S(2)}) %collective-permute-start) | collective-permute-done | bytes 737312 | tf_op jit(solution)/shard_map/ppermute | solution.py:21
  76.5 13.7 %collective-permute-done.4 = bf16[6,128,640]{1,2,0:T(8,128)(2,1)} collective-permute-done((bf16[6,128,640]{1,2,0:T(8,128)(2,1)}, bf16[6,128,640]{1,2,0:T(8,128)(2,1)}, u32[]{:S(2)}, u32[]{:S(2)}) %collective-permute-start.4) | collective-permute-done | bytes 983072 | tf_op jit(solution)/shard_map/ppermute | solution.py:21
  113.0 12.8 %collective-permute-done.12 = bf16[6,128,480]{1,2,0:T(8,128)(2,1)} collective-permute-done((bf16[6,128,480]{1,2,0:T(8,128)(2,1)}, bf16[6,128,480]{1,2,0:T(8,128)(2,1)}, u32[]{:S(2)}, u32[]{:S(2)}) %collective-permute-start.12) | collective-permute-done | bytes 737312 | tf_op jit(solution)/shard_map/ppermute | solution.py:21
  142.8 9.9 %fusion.11 = (f32[6,5,3,128]{3,2,1,0:T(4,128)S(1)}, f32[6,5,512,128,3]{3,2,4,1,0:T(8,128)}) fusion(pred[6,128,512]{1,2,0:T(8,128)(4,1)S(1)} %compare_and_fusion, bf16[6,512,5,64,1]{1,3,4,2,0:T(8,128)(2,1)S(1)} %bitcast.242, bf16[6,128,5,3,32]{1,4,3,2,0:T(8,128)(2,1)S(1)} %bitcast.258, bf16[6,128,5,3,32]{1,4,3,2,0:T(8,128)(2,1)S(1)} %bitcast.256), kind=kOutput, calls=%fused_computation.16 | convolution fusion | flops 775607040 | bytes 27472896 | tf_op jit(solution)/shard_map/sqhgd,skhd->shgqk/dot_general | solution.py:114
  152.7 10.5 %fusion.5 = f32[6,5,3,128]{3,2,1,0:T(4,128)S(1)} fusion(f32[6,5,3,128]{3,2,1,0:T(4,128)S(1)} %get-tuple-element.88, f32[6,5,512,128,3]{3,2,4,1,0:T(8,128)} %get-tuple-element.89, pred[6,128,512]{1,2,0:T(8,128)(4,1)S(1)} %compare_and_fusion), kind=kLoop, calls=%fused_computation.11 | loop fusion | flops 23581440 | bytes 24078336 | tf_op jit(solution)/shard_map/reduce_sum | solution.py:214
  163.2 11.4 %fusion.50 = bf16[6,5,64,3,128]{4,2,3,1,0:T(8,128)(2,1)S(1)} fusion(bf16[6,512,5,64,1]{1,3,4,2,0:T(8,128)(2,1)S(1)} %bitcast.245, f32[6,5,3,128]{3,2,1,0:T(4,128)S(1)} %fusion.5, f32[6,5,3,128]{3,2,1,0:T(4,128)S(1)} %get-tuple-element.88, f32[6,5,512,128,3]{3,2,4,1,0:T(8,128)} %get-tuple-element.89, pred[6,128,512]{1,2,0:T(8,128)(4,1)S(1)} %compare_and_fusion), kind=kOutput, calls=%fused_computation.113 | convolution fusion | flops 785203200 | bytes 27518976 | tf_op jit(solution)/shard_map/shgqk,skhd->sqhgd/dot_general | solution.py:84
  185.4 12.7 %maximum_select_fusion = bf16[3,1280,960]{2,1,0:T(8,128)(2,1)S(1)} fusion(bf16[3,1280,480]{2,1,0:T(8,128)(2,1)} %all-gather.3.cloned.1.call-done, bf16[1,1280,480]{2,1,0:T(8,128)(2,1)} %bitcast.269, bf16[1,1280,480]{2,1,0:T(8,128)(2,1)} %bitcast.268, bf16[1,1280,480]{2,1,0:T(8,128)(2,1)} %bitcast.267, pred[]{:T(512)S(6)} %eq.14), kind=kLoop, calls=%fused_computation.17 | loop fusion | flops 62668800 | bytes 14745601 | tf_op jit(solution)/shard_map/jit(_where)/select_n | solution.py:25
  206.6 6.3 multiply_convert_fusion.2
  237.8 7.8 %multiply_convert_fusion.1 = (bf16[768,1280]{1,0:T(8,128)(2,1)S(1)}, bf16[768,1280]{1,0:T(8,128)(2,1)}, bf16[768,1280]{1,0:T(8,128)(2,1)S(1)}) fusion(f32[768,1280]{1,0:T(8,128)} %fusion.46, f32[768,1280]{1,0:T(8,128)} %fusion.44, bf16[768,960]{0,1:T(8,128)(2,1)} %collective-permute-done.9, bf16[3,1280,960]{2,1,0:T(8,128)(2,1)S(1)} %maximum_select_fusion), kind=kOutput, calls=%fused_computation.33 | convolution fusion | flops 1903165440 | bytes 17858560 | tf_op jit(solution)/shard_map/td,fd->tf/dot_general | solution.py:84
  290.0 9.0 %fusion.112 = (bf16[6,128,960]{1,2,0:T(8,128)(2,1)S(1)}, f32[6,128,960]{1,2,0:T(8,128)}) fusion(f32[6,128,960]{1,2,0:T(8,128)} %copy.121, bf16[6,128,960]{1,2,0:T(8,128)(2,1)} %copy-done.23, f32[960]{0:T(1024)S(1)} %bitcast.295, bf16[6,128,480]{1,2,0:T(8,128)(2,1)S(1)} %get-tuple-element.65, bf16[6,128,480]{1,2,0:T(8,128)(2,1)} %copy-done.12, ...), kind=kOutput, calls=%fused_computation.241 | output fusion | flops 32442048 | bytes 11806465 | tf_op jit(solution)/shard_map/mul | solution.py:78
  301.8 16.4 %fusion.2 = (f32[6,5,3,128]{3,2,1,0:T(4,128)}, f32[6,5,512,128,3]{3,2,4,1,0:T(8,128)}) fusion(f32[6,5,3,128]{3,2,1,0:T(4,128)S(1)} %log_add_fusion, f32[6,5,512,128,3]{3,2,4,1,0:T(8,128)} %get-tuple-element.89, pred[6,128,512]{1,2,0:T(8,128)(4,1)S(1)} %compare_and_fusion, bf16[6,512,5,64,1]{1,3,4,2,0:T(8,128)(2,1)S(1)} %bitcast.246, ...), kind=kOutput, calls=%fused_computation.4 | convolution fusion | flops 784454400 | bytes 51111936 | tf_op jit(solution)/shard_map/sqhgd,skhd->shgqk/dot_general | solution.py:84
  318.2 18.7 %collective-permute-done.24 = bf16[1280,480]{0,1:T(8,128)(2,1)} collective-permute-done((bf16[1280,480]{0,1:T(8,128)(2,1)}, bf16[1280,480]{0,1:T(8,128)(2,1)}, u32[]{:S(2)}, u32[]{:S(2)}) %collective-permute-start.24) | collective-permute-done | bytes 1228832 | tf_op jit(solution)/shard_map/ppermute | solution.py:21
  340.9 11.7 %bitcast_convert_fusion = bf16[6,5,64,512]{3,2,1,0:T(8,128)(2,1)} fusion(bf16[6,128,5,3,64]{1,4,3,2,0:T(8,128)(2,1)S(1)} %bitcast.271, f32[6,5,3,128]{3,2,1,0:T(4,128)S(1)} %log_add_fusion, f32[6,5,512,128,3]{3,2,4,1,0:T(8,128)} %get-tuple-element.89, pred[6,128,512]{1,2,0:T(8,128)(4,1)S(1)} %compare_and_fusion), kind=kOutput, calls=%fused_computation.28 | convolution fusion | flops 779550720 | bytes 27472896 | tf_op jit(solution)/shard_map/shgqk,sqhgd->skhd/dot_general | solution.py:84
  365.2 20.6 %fusion.4 = bf16[6,5,3,128,512]{3,4,2,1,0:T(8,128)(2,1)} fusion(f32[6,5,512,128,3]{3,2,4,1,0:T(8,128)} %get-tuple-element.95, f32[6,5,3,128]{3,2,1,0:T(4,128)} %get-tuple-element.94, f32[6,5,3,128]{3,2,1,0:T(4,128)S(1)} %log_add_fusion, f32[6,5,512,128,3]{3,2,4,1,0:T(8,128)} %get-tuple-element.89, pred[6,128,512]{1,2,0:T(8,128)(4,1)S(1)} %compare_and_fusion), kind=kLoop, calls=%fused_computation.6 | loop fusion | flops 35389440 | bytes 59467776 | tf_op jit(solution)/shard_map/convert_element_type | solution.py:282
  385.9 9.8 %fusion.12 = bf16[6,5,64,512]{3,2,1,0:T(8,128)(2,1)} fusion(bf16[6,5,3,128,512]{3,4,2,1,0:T(8,128)(2,1)} %fusion.4, bf16[6,128,5,3,32]{1,4,3,2,0:T(8,128)(2,1)S(1)} %bitcast.259, bf16[6,128,5,3,32]{1,4,3,2,0:T(8,128)(2,1)S(1)} %bitcast.257), kind=kOutput, calls=%fused_computation.30 | convolution fusion | flops 759889920 | bytes 15237120 | tf_op jit(solution)/shard_map/shgqk,sqhgd->skhd/dot_general | solution.py:84
  402.4 6.6 convolution_multiply_fusion
  429.3 14.4 %collective-permute-done.16 = bf16[6,128,640]{2,1,0:T(8,128)(2,1)S(1)} collective-permute-done((bf16[6,128,640]{2,1,0:T(8,128)(2,1)S(1)}, bf16[6,128,640]{2,1,0:T(8,128)(2,1)S(1)}, u32[]{:S(2)}, u32[]{:S(2)}) %collective-permute-start.16) | collective-permute-done | bytes 983072 | tf_op jit(solution)/shard_map/ppermute | solution.py:21
  459.6 26.3 %collective-permute-done.21 = bf16[240,640]{1,0:T(8,128)(2,1)} collective-permute-done((bf16[240,640]{1,0:T(8,128)(2,1)S(1)}, bf16[240,640]{1,0:T(8,128)(2,1)}, u32[]{:S(2)}, u32[]{:S(2)}) %collective-permute-start.21) | collective-permute-done | bytes 307232 | tf_op jit(solution)/shard_map/ppermute | solution.py:21
  499.1 6.1 fusion.52
  524.9 63.2 %psum.7 = f32[2,960]{1,0:T(2,128)S(1)} all-reduce(f32[2,960]{1,0:T(2,128)S(1)} %pad_maximum_fusion.16), channel_id=1, replica_groups=mesh['dp'=8,'row'=2,'col'=2] {'dp','row','col'}, use_global_device_ids=true, to_apply=%region_9.10 | all-reduce | flops 1920 | bytes 15360 | tf_op jit(solution)/shard_map/psum | solution.py:323
  594.0 31.3 %all_gather.14 = bf16[240,640]{0,1:T(8,128)(2,1)S(1)} all-gather(bf16[240,80]{0,1:T(8,128)(2,1)} %bitcast.293), channel_id=1, replica_groups=mesh['dp'=8,'row'=2,'col'=2] {'dp'}, dimensions={1}, use_global_device_ids=true | all-gather | bytes 345600 | tf_op jit(solution)/shard_map/all_gather | solution.py:67
  626.2 35.6 %all_gather.13 = bf16[240,1920]{0,1:T(8,128)(2,1)S(1)} all-gather(bf16[240,240]{0,1:T(8,128)(2,1)} %bitcast.292), channel_id=1, replica_groups=mesh['dp'=8,'row'=2,'col'=2] {'dp'}, dimensions={1}, use_global_device_ids=true | all-gather | bytes 1036800 | tf_op jit(solution)/shard_map/all_gather | solution.py:67
  664.5 31.8 %all-gather.5.cloned.1.call-done = bf16[3840,480]{1,0:T(8,128)(2,1)} async-done(((bf16[480,480]{1,0:T(8,128)(2,1)}), bf16[3840,480]{1,0:T(8,128)(2,1)}) %all-gather.5.cloned.1.call-update) | async-done | bytes 3686416 | tf_op jit(solution)/shard_map/all_gather | solution.py:67
  (335 shorter events, 282.2 us)
Async XLA Ops:
  7.2 178.2 %all-gather.3.cloned.1.call-start = ((), (), s32[]{:S(2)}) async-start(), calls=%async_computation.3 | async-start | bytes 4423680 | tf_op jit(solution)/shard_map/all_gather | solution.py:166
  14.3 23.9 %collective-permute-start.1 = (f32[2,480]{1,0:T(2,128)S(1)}, f32[2,480]{1,0:T(2,128)S(1)}, u32[]{:S(2)}, u32[]{:S(2)}) collective-permute-start(f32[2,480]{1,0:T(2,128)S(1)} %pad_maximum_fusion.17), channel_id=1, source_target_pairs={{0,2},{2,0},{1,3},{3,1},{4,6},{6,4},{5,7},{7,5},{8,10},{10,8},{9,1... | collective-permute-start | bytes 11528 | tf_op jit(solution)/shard_map/ppermute | solution.py:21
  65.2 25.0 %collective-permute-start.4 = (bf16[6,128,640]{1,2,0:T(8,128)(2,1)}, bf16[6,128,640]{1,2,0:T(8,128)(2,1)}, u32[]{:S(2)}, u32[]{:S(2)}) collective-permute-start(bf16[6,128,640]{1,2,0:T(8,128)(2,1)} %pad_maximum_fusion.7), channel_id=1, source_target_pairs={{0,2},{2,0},{1,3},{3,1},{4,6},{6,4},{5,7},{7,5},{8,10},{10,8},{9,1... | collective-permute-start | bytes 2949128 | tf_op jit(solution)/shard_map/ppermute | solution.py:21
  66.9 33.8 %collective-permute-start.6 = (bf16[240,960]{1,0:T(8,128)(2,1)}, bf16[240,960]{1,0:T(8,128)(2,1)}, u32[]{:S(2)}, u32[]{:S(2)}) collective-permute-start(bf16[240,960]{1,0:T(8,128)(2,1)} %param.20), channel_id=1, source_target_pairs={{0,2},{2,0},{1,3},{3,1},{4,6},{6,4},{5,7},{7,5},{8,10},{10,8},{9,1... | collective-permute-start | bytes 1382408 | tf_op jit(solution)/shard_map/ppermute | solution.py:21
  74.8 36.5 %collective-permute-start.8 = (bf16[3,160,480]{2,1,0:T(8,128)(2,1)}, bf16[3,160,480]{2,1,0:T(8,128)(2,1)}, u32[]{:S(2)}, u32[]{:S(2)}) collective-permute-start(bf16[3,160,480]{2,1,0:T(8,128)(2,1)} %pad_maximum_fusion.14), channel_id=1, source_target_pairs={{0,2},{2,0},{1,3},{3,1},{4,6},{6,4},{5,7},{7,5},{8,10},{10,8},{9,1... | collective-permute-start | bytes 1382408 | tf_op jit(solution)/shard_map/ppermute | solution.py:21
  92.9 47.1 %collective-permute-start.5 = (bf16[6,256,640]{1,2,0:T(8,128)(2,1)}, bf16[6,256,640]{1,2,0:T(8,128)(2,1)}, u32[]{:S(2)}, u32[]{:S(2)}) collective-permute-start(bf16[6,256,640]{1,2,0:T(8,128)(2,1)} %pad_maximum_fusion.4), channel_id=1, source_target_pairs={{0,1},{1,0},{2,3},{3,2},{4,5},{5,4},{6,7},{7,6},{8,9},{9,8},{10,11... | collective-permute-start | bytes 5898248 | tf_op jit(solution)/shard_map/ppermute | solution.py:21
  94.0 31.8 %collective-permute-start.12 = (bf16[6,128,480]{1,2,0:T(8,128)(2,1)}, bf16[6,128,480]{1,2,0:T(8,128)(2,1)}, u32[]{:S(2)}, u32[]{:S(2)}) collective-permute-start(bf16[6,128,480]{1,2,0:T(8,128)(2,1)} %get-tuple-element.61), channel_id=1, source_target_pairs={{0,2},{2,0},{1,3},{3,1},{4,6},{6,4},{5,7},{7,5},{8,10},{10,8},{9,1... | collective-permute-start | bytes 2211848 | tf_op jit(solution)/shard_map/ppermute | solution.py:21
  103.3 31.8 %collective-permute-start.7 = (bf16[2,240,960]{2,1,0:T(8,128)(2,1)}, bf16[2,240,960]{2,1,0:T(8,128)(2,1)}, u32[]{:S(2)}, u32[]{:S(2)}) collective-permute-start(bf16[2,240,960]{2,1,0:T(8,128)(2,1)} %maximum_select_fusion.11), channel_id=1, source_target_pairs={{0,1},{1,0},{2,3},{3,2},{4,5},{5,4},{6,7},{7,6},{8,9},{9,8},{10,11... | collective-permute-start | bytes 2764808 | tf_op jit(solution)/shard_map/ppermute | solution.py:21
  111.3 384.6 %reduce-scatter.14.cloned.1.call-start = ((), (), s32[]{:S(2)}) async-start(), calls=%async_computation.7 | async-start | bytes 4423680 | tf_op jit(solution)/shard_map/reduce_scatter | solution.py:64
  135.1 91.1 %collective-permute-start.13 = (bf16[768,960]{0,1:T(8,128)(2,1)}, bf16[768,960]{0,1:T(8,128)(2,1)}, u32[]{:S(2)}, u32[]{:S(2)}) collective-permute-start(bf16[768,960]{0,1:T(8,128)(2,1)} %copy.119), channel_id=1, source_target_pairs={{0,1},{1,0},{2,3},{3,2},{4,5},{5,4},{6,7},{7,6},{8,9},{9,8},{10,11... | collective-permute-start | bytes 4423688 | tf_op jit(solution)/shard_map/ppermute | solution.py:21
  184.9 46.9 %collective-permute-start.9 = (bf16[768,960]{0,1:T(8,128)(2,1)}, bf16[768,960]{0,1:T(8,128)(2,1)}, u32[]{:S(2)}, u32[]{:S(2)}) collective-permute-start(bf16[768,960]{0,1:T(8,128)(2,1)} %copy.114), channel_id=1, source_target_pairs={{0,1},{1,0},{2,3},{3,2},{4,5},{5,4},{6,7},{7,6},{8,9},{9,8},{10,11... | collective-permute-start | bytes 4423688 | tf_op jit(solution)/shard_map/ppermute | solution.py:21
  250.2 30.8 %collective-permute-start.14 = (bf16[768,960]{0,1:T(8,128)(2,1)S(1)}, bf16[768,960]{0,1:T(8,128)(2,1)S(1)}, u32[]{:S(2)}, u32[]{:S(2)}) collective-permute-start(bf16[768,960]{0,1:T(8,128)(2,1)S(1)} %add_convert_fusion.2), channel_id=1, source_target_pairs={{0,1},{1,0},{2,3},{3,2},{4,5},{5,4},{6,7},{7,6},{8,9},{9,8},{10,11... | collective-permute-start | bytes 4423688 | tf_op jit(solution)/shard_map/ppermute | solution.py:21
  254.5 98.2 %collective-permute-start.23 = (bf16[1280,480]{0,1:T(8,128)(2,1)}, bf16[1280,480]{0,1:T(8,128)(2,1)}, u32[]{:S(2)}, u32[]{:S(2)}) collective-permute-start(bf16[1280,480]{0,1:T(8,128)(2,1)} %fusion.26), channel_id=1, source_target_pairs={{0,2},{2,0},{1,3},{3,1},{4,6},{6,4},{5,7},{7,5},{8,10},{10,8},{9,1... | collective-permute-start | bytes 3686408 | tf_op jit(solution)/shard_map/ppermute | solution.py:21
  259.5 79.7 %collective-permute-start.22 = (bf16[1280,480]{0,1:T(8,128)(2,1)}, bf16[1280,480]{0,1:T(8,128)(2,1)}, u32[]{:S(2)}, u32[]{:S(2)}) collective-permute-start(bf16[1280,480]{0,1:T(8,128)(2,1)} %fusion.25), channel_id=1, source_target_pairs={{0,2},{2,0},{1,3},{3,1},{4,6},{6,4},{5,7},{7,5},{8,10},{10,8},{9,1... | collective-permute-start | bytes 3686408 | tf_op jit(solution)/shard_map/ppermute | solution.py:21
  263.5 73.4 %collective-permute-start.24 = (bf16[1280,480]{0,1:T(8,128)(2,1)}, bf16[1280,480]{0,1:T(8,128)(2,1)}, u32[]{:S(2)}, u32[]{:S(2)}) collective-permute-start(bf16[1280,480]{0,1:T(8,128)(2,1)} %fusion.27), channel_id=1, source_target_pairs={{0,2},{2,0},{1,3},{3,1},{4,6},{6,4},{5,7},{7,5},{8,10},{10,8},{9,1... | collective-permute-start | bytes 3686408 | tf_op jit(solution)/shard_map/ppermute | solution.py:21
  362.2 231.7 %reduce-scatter.12.cloned.1.call-start = ((), (), s32[]{:S(2)}) async-start(), calls=%async_computation.6 | async-start | bytes 368640
  419.6 24.1 %collective-permute-start.16 = (bf16[6,128,640]{2,1,0:T(8,128)(2,1)S(1)}, bf16[6,128,640]{2,1,0:T(8,128)(2,1)S(1)}, u32[]{:S(2)}, u32[]{:S(2)}) collective-permute-start(bf16[6,128,640]{2,1,0:T(8,128)(2,1)S(1)} %slice.237), channel_id=1, source_target_pairs={{0,2},{2,0},{1,3},{3,1},{4,6},{6,4},{5,7},{7,5},{8,10},{10,8},{9,1... | collective-permute-start | bytes 2949128 | tf_op jit(solution)/shard_map/ppermute | solution.py:21
  429.1 25.1 %collective-permute-start.18 = (bf16[2,240,1920]{2,1,0:T(8,128)(2,1)}, bf16[2,240,1920]{2,1,0:T(8,128)(2,1)}, u32[]{:S(2)}, u32[]{:S(2)}) collective-permute-start(bf16[2,240,1920]{2,1,0:T(8,128)(2,1)} %fusion.36), channel_id=1, source_target_pairs={{0,1},{1,0},{2,3},{3,2},{4,5},{5,4},{6,7},{7,6},{8,9},{9,8},{10,11... | collective-permute-start | bytes 5529608 | tf_op jit(solution)/shard_map/ppermute | solution.py:21
  456.2 31.9 %collective-permute-start.19 = (bf16[240,1920]{1,0:T(8,128)(2,1)S(1)}, bf16[240,1920]{1,0:T(8,128)(2,1)S(1)}, u32[]{:S(2)}, u32[]{:S(2)}) collective-permute-start(bf16[240,1920]{1,0:T(8,128)(2,1)S(1)} %fusion.59), channel_id=1, source_target_pairs={{0,2},{2,0},{1,3},{3,1},{4,6},{6,4},{5,7},{7,5},{8,10},{10,8},{9,1... | collective-permute-start | bytes 2764808 | tf_op jit(solution)/shard_map/ppermute | solution.py:21
  458.1 27.7 %collective-permute-start.21 = (bf16[240,640]{1,0:T(8,128)(2,1)S(1)}, bf16[240,640]{1,0:T(8,128)(2,1)}, u32[]{:S(2)}, u32[]{:S(2)}) collective-permute-start(bf16[240,640]{1,0:T(8,128)(2,1)S(1)} %fusion.81), channel_id=1, source_target_pairs={{0,2},{2,0},{1,3},{3,1},{4,6},{6,4},{5,7},{7,5},{8,10},{10,8},{9,1... | collective-permute-start | bytes 921608 | tf_op jit(solution)/shard_map/ppermute | solution.py:21
  487.8 138.3 %reduce-scatter.10.cloned.1.call-start = ((), (), s32[]{:S(2)}) async-start(), calls=%async_computation.5 | async-start | bytes 1105920
  491.2 205.1 %all-gather.5.cloned.1.call-start = ((), (), s32[]{:S(2)}) async-start(), calls=%async_computation.4 | async-start | bytes 4423680 | tf_op jit(solution)/shard_map/all_gather | solution.py:67
  518.6 70.2 %collective-permute-start.11 = (bf16[6,128,480]{1,2,0:T(8,128)(2,1)S(1)}, bf16[6,128,480]{1,2,0:T(8,128)(2,1)}, u32[]{:S(2)}, u32[]{:S(2)}) collective-permute-start(bf16[6,128,480]{1,2,0:T(8,128)(2,1)S(1)} %get-tuple-element.63), channel_id=1, source_target_pairs={{0,2},{2,0},{1,3},{3,1},{4,6},{6,4},{5,7},{7,5},{8,10},{10,8},{9,1... | collective-permute-start | bytes 2211848 | tf_op jit(solution)/shard_map/ppermute | solution.py:21
  523.3 68.5 %collective-permute-start.17 = (bf16[6,128,480]{1,2,0:T(8,128)(2,1)}, bf16[6,128,480]{1,2,0:T(8,128)(2,1)S(1)}, u32[]{:S(2)}, u32[]{:S(2)}) collective-permute-start(bf16[6,128,480]{1,2,0:T(8,128)(2,1)} %get-tuple-element.59), channel_id=1, source_target_pairs={{0,2},{2,0},{1,3},{3,1},{4,6},{6,4},{5,7},{7,5},{8,10},{10,8},{9,1... | collective-permute-start | bytes 2211848 | tf_op jit(solution)/shard_map/ppermute | solution.py:21
  (78 other events, 1145.4 us)
Sparse Core Ops, SparseCore 0:
  111.4 71.5 all-gather.2
  362.4 85.6 reduce-scatter.13
  488.0 62.7 reduce-scatter.11
  554.9 62.3 reduce-scatter.9
  619.3 76.9 all-gather.4

commit v2 on v1

--- a/solution.py
+++ b/solution.py
@@ -65,6 +65,45 @@
         values.astype(jnp.bfloat16), "dp", scatter_dimension=dim, tiled=True
     )
     return lax.all_gather(part, "dp", axis=dim, tiled=True)
+
+
+def xor_partner(values, step):
+    size = lax.axis_size("dp")
+    return lax.ppermute(values, "dp", [(i, i ^ step) for i in range(size)])
+
+
+def dp_direct(values):
+    size = lax.axis_size("dp")
+    rows = values.shape[0]
+    if size > 8 or size & (size - 1) or rows % size:
+        return dp_total(values, 1)
+    index = lax.axis_index("dp")
+    piece = rows // size
+    values = values.astype(jnp.bfloat16)
+
+    def piece_of(step):
+        return lax.dynamic_slice_in_dim(values, (index ^ step) * piece, piece, 0)
+
+    total = piece_of(0).astype(jnp.float32)
+    for part in [xor_partner(piece_of(step), step) for step in range(1, size)]:
+        total = total + part.astype(jnp.float32)
+    total = total.astype(jnp.bfloat16)
+    pieces = jnp.stack([total] + [xor_partner(total, step) for step in range(1, size)])
+    return jnp.concatenate(
+        [lax.dynamic_index_in_dim(pieces, index ^ j, 0, keepdims=False) for j in range(size)],
+        axis=0,
+    )
+
+
+def dp_small(values):
+    size = lax.axis_size("dp")
+    if size & (size - 1):
+        return lax.psum(values, "dp")
+    step = 1
+    while step < size:
+        values = values + xor_partner(values, step)
+        step *= 2
+    return values
 
 
 def norm_apply(values, gain):
@@ -148,10 +187,6 @@
     col_index = lax.axis_index("col")
     bf16 = jnp.bfloat16
 
-    x_tok = to_tokens(inputs, row_index).astype(jnp.float32)
-    qkv_full = gather_rows(
-        jnp.concatenate([query_weight, key_weight, value_weight], axis=1), row_index, col_index
-    )
 
     own_ffn = jnp.stack([gate_weight.T, up_weight.T, down_weight])
     units = own_ffn.shape[1]
@@ -163,13 +198,18 @@
             lax.dynamic_slice_in_dim(down_weight, dp_index * piece, piece, 0),
         ]
     )
-    other_ffn = lax.all_gather(swap(ffn_slice, "row"), "dp", axis=1, tiled=True)
+    x_tok, other_slice = lax.optimization_barrier(
+        (to_tokens(inputs, row_index), swap(ffn_slice, "row"))
+    )
+    x_tok = x_tok.astype(jnp.float32)
+    qkv_full = gather_rows(
+        jnp.concatenate([query_weight, key_weight, value_weight], axis=1), row_index, col_index
+    )
+    other_ffn = lax.all_gather(other_slice, "dp", axis=1, tiled=True)
     ffn_full = ordered(own_ffn, other_ffn, row_index, 2)
     gate_full, up_full, down_full = ffn_full[0], ffn_full[1], ffn_full[2]
-    output_full = gather_rows(output_weight, row_index, col_index)
     gain_own = jnp.stack([gain_first, gain_second])
     gain_full = ordered(gain_own, swap(gain_own, "row"), row_index, 1)
-    dy_own = to_tokens(cotangent, row_index)
 
     starts = [
         (c * 2 + r) * quarter
@@ -202,6 +242,11 @@
         [key_rot.reshape(seq_count, quarter, KD), qkv_lin[..., QD + KD :].astype(bf16)], axis=2
     )
     kv_pair = jnp.concatenate([kv_own, swap(kv_own, "row")], axis=1)
+    kv_pair, later_weight, later_dy = lax.optimization_barrier(
+        (kv_pair, output_weight, cotangent)
+    )
+    output_full = gather_rows(later_weight, row_index, col_index)
+    dy_own = to_tokens(later_dy, row_index)
     kv_all = jnp.concatenate([kv_pair, swap(kv_pair, "col")], axis=1)
     query_rot = rotate(
         qkv_lin[..., :QD].reshape(seq_count, quarter, QH, HD), cosine, sine_term
@@ -318,10 +363,11 @@
 
     ffn_sum = dp_total(ffn_part, 0).astype(jnp.float32)
     qo_part = jnp.concatenate([query_part, output_part], axis=1)
-    qo_sum = dp_total(scatter_rows(qo_part, row_index, col_index), 1).astype(jnp.float32)
-    kv_grad = dp_total(scatter_rows(kv_part, row_index, col_index), 1).astype(jnp.float32)
-    gain_sum = lax.psum(jnp.stack([gain_first_part, gain_second_part]), ("dp", "row", "col"))
-    gain_sum = half_of(gain_sum, row_index, 1)
+    qo_sum = dp_direct(scatter_rows(qo_part, row_index, col_index)).astype(jnp.float32)
+    kv_grad = dp_direct(scatter_rows(kv_part, row_index, col_index)).astype(jnp.float32)
+    gain_part = jnp.stack([gain_first_part, gain_second_part])
+    gain_sum = half_of(gain_part, row_index, 1) + swap(half_of(gain_part, 1 - row_index, 1), "row")
+    gain_sum = dp_small(gain_sum + swap(gain_sum, "col"))
     return (
         layer_out,
         input_grad,

time: 727 us -> 646 us (0.89)
  blocking collectives: 130 us -> 0 us
  starting transfers between devices: 23.8 us -> 91 us
  waiting for transfers between devices: 163 us -> 122 us
  local copies, waits for them, and re-layouts: 91.2 us -> 113 us
    ppermute x0 -> x31, starting transfers between devices: none -> 68.7 us  [xor_partner(): return lax.ppermute(values, 'dp', [(i, i ^ step) for i in range(size)])]
    all_gather x2 -> x0, blocking collectives: 66.9 us -> none  [dp_total(): return lax.all_gather(part, 'dp', axis=dim, tiled=True)]
    psum x1 -> x0, blocking collectives: 63.2 us -> none  [local(): lax.psum(jnp.stack([gain_first_part, gain_second_part]), ('dp', 'row', 'c...]
    ppermute x25 -> x27, waiting for transfers between devices: 131 us -> 98.3 us  [swap(): lax.ppermute(values, axis_name, [(i, size - 1 - i) for i in range(size)])]
    all_gather x1, waiting for transfers between devices: 31.8 us -> 0.01 us  [dp_total(): return lax.all_gather(part, 'dp', axis=dim, tiled=True)]
    ppermute x0 -> x31, waiting for transfers between devices: none -> 18.5 us  [xor_partner(): return lax.ppermute(values, 'dp', [(i, i ^ step) for i in range(size)])]
    concatenate x0 -> x3, local copies, waits for them, and re-layouts: none -> 7.5 us  [the longest x2 5.79 us: dp_direct(): jnp.concatenate([lax.dynamic_index_in_dim(pieces, index ^ j, 0, keepdims=...]
    unnamed x155 -> x156, local copies, waits for them, and re-layouts: 38.8 us -> 43.2 us
  transfers between devices with their start and end apart: 30 -> 61, of which waited for: 11 -> 18; matrix products, arithmetic and copies ran while one was open for 44% -> 55% of each run, Pallas kernels for 0% -> 0%
where the time goes in v2:
time: 646 us; the launch traced here: 637 us
  matrix products  179 us (28%)
  waiting for transfers between devices  122 us (19%)
  other arithmetic  117 us (18%)
  local copies, waits for them, and re-layouts  113 us (17%)
  starting transfers between devices  91 us (14%)
  between operations  15.5 us (2%)
    dot_general x37, matrix products, dot(): return jnp.einsum(spec, left, right, preferred_element_type=jnp.float32)  169 us
    ppermute x27, waiting for transfers between devices, swap(): lax.ppermute(values, axis_name, [(i, size - 1 - i) for i in range(size)])  98.3 us
    ppermute x31, starting transfers between devices, xor_partner(): return lax.ppermute(values, 'dp', [(i, i ^ step) for i in range(size)])  68.7 us
    unnamed x156, local copies, waits for them, and re-layouts  43.2 us
    select_n x11, other arithmetic, ordered(): jnp.where(index == 0, jnp.concatenate([own, other], axis=axis), jnp.conca...  31.4 us
    ppermute x27, starting transfers between devices, swap(): lax.ppermute(values, axis_name, [(i, size - 1 - i) for i in range(size)])  21.9 us
    convert_element_type x1, other arithmetic, local(): grad_scores = (exact_probs * (grad_probs - row_delta)).astype(bf16)  20.4 us
    ppermute x31, waiting for transfers between devices, xor_partner(): return lax.ppermute(values, 'dp', [(i, i ^ step) for i in range(size)])  18.5 us
  transfers between devices with their start and end apart: 61, of which 18 were waited for; matrix products, arithmetic and copies ran while one was open for 55% of the time, Pallas kernels for 0%

profile of v2, /device:TPU:0, one launch (start us, length us, event | category | flops | bytes accessed | tf_op | source)
XLA Modules:
  0.0 637.0 jit_solution(11709156733794711437)
XLA Ops:
  26.6 5.7 collective-permute-done.3
  35.1 22.7 %collective-permute-done = bf16[6,128,480]{1,2,0:T(8,128)(2,1)S(1)} collective-permute-done((bf16[6,128,480]{1,2,0:T(8,128)(2,1)}, bf16[6,128,480]{1,2,0:T(8,128)(2,1)S(1)}, u32[]{:S(2)}, u32[]{:S(2)}) %collective-permute-start) | collective-permute-done | bytes 737312 | tf_op jit(solution)/shard_map/ppermute | solution.py:21
  72.1 21.2 %collective-permute-done.5 = bf16[6,128,640]{1,2,0:T(8,128)(2,1)S(1)} collective-permute-done((bf16[6,128,640]{1,2,0:T(8,128)(2,1)S(1)}, bf16[6,128,640]{1,2,0:T(8,128)(2,1)S(1)}, u32[]{:S(2)}, u32[]{:S(2)}) %collective-permute-start.5) | collective-permute-done | bytes 983072 | tf_op jit(solution)/shard_map/ppermute | solution.py:21
  101.0 9.3 %collective-permute-done.7 = bf16[240,960]{1,0:T(8,128)(2,1)S(1)} collective-permute-done((bf16[240,960]{1,0:T(8,128)(2,1)S(1)}, bf16[240,960]{1,0:T(8,128)(2,1)S(1)}, u32[]{:S(2)}, u32[]{:S(2)}) %collective-permute-start.7) | collective-permute-done | bytes 460832 | tf_op jit(solution)/shard_map/ppermute | solution.py:21
  140.5 10.1 %fusion.11 = (f32[6,5,3,128]{3,2,1,0:T(4,128)S(1)}, f32[6,5,512,128,3]{3,2,4,1,0:T(8,128)}) fusion(pred[6,128,512]{1,2,0:T(8,128)(4,1)S(1)} %compare_and_fusion, bf16[6,512,5,64,1]{1,3,4,2,0:T(8,128)(2,1)S(1)} %bitcast.286, bf16[6,128,5,3,32]{1,4,3,2,0:T(8,128)(2,1)S(1)} %bitcast.299, bf16[6,128,5,3,32]{1,4,3,2,0:T(8,128)(2,1)S(1)} %bitcast.297), kind=kOutput, calls=%fused_computation.16 | convolution fusion | flops 775607040 | bytes 27472896 | tf_op jit(solution)/shard_map/sqhgd,skhd->shgqk/dot_general | solution.py:153
  150.6 10.5 %fusion.5 = f32[6,5,3,128]{3,2,1,0:T(4,128)S(1)} fusion(f32[6,5,3,128]{3,2,1,0:T(4,128)S(1)} %get-tuple-element.121, f32[6,5,512,128,3]{3,2,4,1,0:T(8,128)} %get-tuple-element.122, pred[6,128,512]{1,2,0:T(8,128)(4,1)S(1)} %compare_and_fusion), kind=kLoop, calls=%fused_computation.11 | loop fusion | flops 23581440 | bytes 24078336 | tf_op jit(solution)/shard_map/reduce_sum | solution.py:259
  161.2 11.2 %fusion.50 = bf16[6,5,64,3,128]{4,2,3,1,0:T(8,128)(2,1)S(1)} fusion(bf16[6,512,5,64,1]{1,3,4,2,0:T(8,128)(2,1)S(1)} %bitcast.289, f32[6,5,3,128]{3,2,1,0:T(4,128)S(1)} %fusion.5, f32[6,5,3,128]{3,2,1,0:T(4,128)S(1)} %get-tuple-element.121, f32[6,5,512,128,3]{3,2,4,1,0:T(8,128)} %get-tuple-element.122, pred[6,128,512]{1,2,0:T(8,128)(4,1)S(1)} %compare_and_fusion), kind=kOutput, calls=%fused_computation.112 | convolution fusion | flops 785203200 | bytes 27518976 | tf_op jit(solution)/shard_map/shgqk,skhd->sqhgd/dot_general | solution.py:123
  183.7 12.4 %maximum_select_fusion = bf16[3,1280,960]{2,1,0:T(8,128)(2,1)S(1)} fusion(bf16[3,1280,480]{2,1,0:T(8,128)(2,1)} %all-gather.3.cloned.1.call-done, bf16[1,1280,480]{2,1,0:T(8,128)(2,1)} %bitcast.310, bf16[1,1280,480]{2,1,0:T(8,128)(2,1)} %bitcast.309, bf16[1,1280,480]{2,1,0:T(8,128)(2,1)} %bitcast.308, pred[]{:T(512)S(6)} %eq.14), kind=kLoop, calls=%fused_computation.17 | loop fusion | flops 62668800 | bytes 14745601 | tf_op jit(solution)/shard_map/jit(_where)/select_n | solution.py:25
  204.6 7.5 %multiply_convert_fusion.2 = (bf16[768,1280]{1,0:T(8,128)(2,1)S(1)}, bf16[768,1280]{1,0:T(8,128)(2,1)S(1)}, bf16[768,1280]{1,0:T(8,128)(2,1)}) fusion(f32[768,1280]{1,0:T(8,128)} %fusion.41, f32[768,1280]{1,0:T(8,128)} %fusion.45, bf16[768,960]{1,0:T(8,128)(2,1)S(1)} %copy-done.16, bf16[3,1280,960]{2,1,0:T(8,128)(2,1)S(1)} %maximum_select_fusion), kind=kOutput, calls=%fused_computation.33 | convolution fusion | flops 1903165440 | bytes 17956864 | tf_op jit(solution)/shard_map/td,fd->tf/dot_general | solution.py:123
  223.7 5.6 fusion.40
  229.3 7.6 %multiply_convert_fusion = (bf16[768,1280]{1,0:T(8,128)(2,1)}, bf16[768,1280]{1,0:T(8,128)(2,1)S(1)}, bf16[768,1280]{1,0:T(8,128)(2,1)S(1)}) fusion(f32[768,1280]{1,0:T(8,128)} %fusion.40, f32[768,1280]{1,0:T(8,128)} %fusion.44, bf16[768,960]{0,1:T(8,128)(2,1)} %collective-permute-done.13, bf16[3,1280,960]{2,1,0:T(8,128)(2,1)S(1)} %maximum_select_fusion), kind=kOutput, calls=%fused_computation.31 | convolution fusion | flops 1903165440 | bytes 17858560 | tf_op jit(solution)/shard_map/td,fd->tf/dot_general | solution.py:123
  286.0 7.2 %fusion.115 = (bf16[6,128,960]{1,2,0:T(8,128)(2,1)S(1)}, f32[6,128,960]{1,2,0:T(8,128)}) fusion(f32[6,128,960]{1,2,0:T(8,128)} %copy.92, bf16[6,128,960]{1,2,0:T(8,128)(2,1)S(1)} %copy-done.19, bf16[6,128,960]{1,2,0:T(8,128)(2,1)S(1)} %maximum_select_fusion.6, f32[960]{0:T(1024)S(1)} %bitcast.352, f32[6,128]{1,0:T(8,128)S(1)} %get-tuple-element.119, ...), kind=kOutput, calls=%fused_computation.295 | output fusion | flops 19171008 | bytes 11806465 | tf_op jit(solution)/shard_map/mul | solution.py:117
  298.5 12.0 %bitcast_convert_fusion = bf16[6,5,64,512]{3,2,1,0:T(8,128)(2,1)} fusion(bf16[6,128,5,3,64]{1,4,3,2,0:T(8,128)(2,1)S(1)} %bitcast.313, f32[6,5,3,128]{3,2,1,0:T(4,128)S(1)} %log_add_fusion, f32[6,5,512,128,3]{3,2,4,1,0:T(8,128)} %get-tuple-element.122, pred[6,128,512]{1,2,0:T(8,128)(4,1)S(1)} %compare_and_fusion), kind=kOutput, calls=%fused_computation.27 | convolution fusion | flops 779550720 | bytes 27472896 | tf_op jit(solution)/shard_map/shgqk,sqhgd->skhd/dot_general | solution.py:123
  310.5 21.1 %fusion.2 = (f32[6,5,3,128]{3,2,1,0:T(4,128)S(1)}, f32[6,5,512,128,3]{3,2,4,1,0:T(8,128)}) fusion(f32[6,5,3,128]{3,2,1,0:T(4,128)S(1)} %log_add_fusion, f32[6,5,512,128,3]{3,2,4,1,0:T(8,128)} %get-tuple-element.122, pred[6,128,512]{1,2,0:T(8,128)(4,1)S(1)} %compare_and_fusion, bf16[6,512,5,64,1]{1,3,4,2,0:T(8,128)(2,1)} %bitcast.290, ...), kind=kOutput, calls=%fused_computation.4 | convolution fusion | flops 784454400 | bytes 51111936 | tf_op jit(solution)/shard_map/sqhgd,skhd->shgqk/dot_general | solution.py:123
  331.6 20.4 %fusion.4 = bf16[6,5,3,128,512]{3,4,2,1,0:T(8,128)(2,1)} fusion(f32[6,5,512,128,3]{3,2,4,1,0:T(8,128)} %get-tuple-element.128, f32[6,5,3,128]{3,2,1,0:T(4,128)S(1)} %get-tuple-element.127, f32[6,5,3,128]{3,2,1,0:T(4,128)S(1)} %log_add_fusion, f32[6,5,512,128,3]{3,2,4,1,0:T(8,128)} %get-tuple-element.122, pred[6,128,512]{1,2,0:T(8,128)(4,1)S(1)} %compare_and_fusion), kind=kLoop, calls=%fused_computation.6 | loop fusion | flops 35389440 | bytes 59467776 | tf_op jit(solution)/shard_map/convert_element_type | solution.py:327
  352.0 8.4 %fusion.12 = bf16[6,5,64,512]{3,2,1,0:T(8,128)(2,1)S(1)} fusion(bf16[6,5,3,128,512]{3,4,2,1,0:T(8,128)(2,1)} %fusion.4, bf16[6,128,5,3,32]{1,4,3,2,0:T(8,128)(2,1)S(1)} %bitcast.300, bf16[6,128,5,3,32]{1,4,3,2,0:T(8,128)(2,1)S(1)} %bitcast.298), kind=kOutput, calls=%fused_computation.29 | convolution fusion | flops 759889920 | bytes 15237120 | tf_op jit(solution)/shard_map/shgqk,sqhgd->skhd/dot_general | solution.py:123
  360.4 8.0 %convolution_multiply_fusion = f32[6,5,64,3,128]{4,2,3,1,0:T(8,128)} fusion(bf16[6,512,5,64,1]{1,3,4,2,0:T(8,128)(2,1)S(1)} %bitcast.287, bf16[6,5,3,128,512]{3,4,2,1,0:T(8,128)(2,1)} %fusion.4), kind=kOutput, calls=%fused_computation.99 | convolution fusion | flops 755712000 | bytes 16711680 | tf_op jit(solution)/shard_map/shgqk,skhd->sqhgd/dot_general | solution.py:123
  399.1 6.2 copy.123
  405.3 5.6 fusion.51
  411.3 8.1 %collective-permute-done.24 = bf16[240,1920]{1,0:T(8,128)(2,1)S(1)} collective-permute-done((bf16[240,1920]{1,0:T(8,128)(2,1)S(1)}, bf16[240,1920]{1,0:T(8,128)(2,1)S(1)}, u32[]{:S(2)}, u32[]{:S(2)}) %collective-permute-start.24) | collective-permute-done | bytes 921632 | tf_op jit(solution)/shard_map/ppermute | solution.py:21
  436.2 13.3 %collective-permute-start.27 = (bf16[30,1920]{1,0:T(8,128)(2,1)}, bf16[30,1920]{1,0:T(8,128)(2,1)}, u32[]{:S(2)}, u32[]{:S(2)}) collective-permute-start(bf16[30,1920]{1,0:T(8,128)(2,1)} %get-tuple-element.88), channel_id=1, source_target_pairs={{0,12},{4,8},{8,4},{12,0},{16,28},{20,24},{24,20},{28,16},{1,13},{... | collective-permute-start | bytes 345608 | tf_op jit(solution)/shard_map/ppermute | solution.py:72
  449.5 6.0 collective-permute-start.26
  455.5 6.0 fusion.52
  537.9 27.0 %collective-permute-done.40 = bf16[240,640]{1,0:T(8,128)(2,1)} collective-permute-done((bf16[240,640]{1,0:T(8,128)(2,1)}, bf16[240,640]{1,0:T(8,128)(2,1)}, u32[]{:S(2)}, u32[]{:S(2)}) %collective-permute-start.40) | collective-permute-done | bytes 307232 | tf_op jit(solution)/shard_map/ppermute | solution.py:21
  (415 shorter events, 348.6 us)
Async XLA Ops:
  7.2 176.5 %all-gather.3.cloned.1.call-start = ((), (), s32[]{:S(2)}) async-start(), calls=%async_computation.1 | async-start | bytes 4423680 | tf_op jit(solution)/shard_map/all_gather | solution.py:208
  21.9 39.0 %collective-permute-start.1 = (bf16[3,160,480]{2,1,0:T(8,128)(2,1)}, bf16[3,160,480]{2,1,0:T(8,128)(2,1)}, u32[]{:S(2)}, u32[]{:S(2)}) collective-permute-start(bf16[3,160,480]{2,1,0:T(8,128)(2,1)} %pad_maximum_fusion.12), channel_id=1, source_target_pairs={{0,2},{2,0},{1,3},{3,1},{4,6},{6,4},{5,7},{7,5},{8,10},{10,8},{9,1... | collective-permute-start | bytes 1382408 | tf_op jit(solution)/shard_map/ppermute | solution.py:21
  26.5 31.3 %collective-permute-start = (bf16[6,128,480]{1,2,0:T(8,128)(2,1)}, bf16[6,128,480]{1,2,0:T(8,128)(2,1)S(1)}, u32[]{:S(2)}, u32[]{:S(2)}) collective-permute-start(bf16[6,128,480]{1,2,0:T(8,128)(2,1)} %get-tuple-element.68), channel_id=1, source_target_pairs={{0,2},{2,0},{1,3},{3,1},{4,6},{6,4},{5,7},{7,5},{8,10},{10,8},{9,1... | collective-permute-start | bytes 2211848 | tf_op jit(solution)/shard_map/ppermute | solution.py:21
  94.8 43.1 %collective-permute-start.6 = (bf16[6,256,640]{1,2,0:T(8,128)(2,1)}, bf16[6,256,640]{1,2,0:T(8,128)(2,1)}, u32[]{:S(2)}, u32[]{:S(2)}) collective-permute-start(bf16[6,256,640]{1,2,0:T(8,128)(2,1)} %pad_maximum_fusion.3), channel_id=1, source_target_pairs={{0,1},{1,0},{2,3},{3,2},{4,5},{5,4},{6,7},{7,6},{8,9},{9,8},{10,11... | collective-permute-start | bytes 5898248 | tf_op jit(solution)/shard_map/ppermute | solution.py:21
  112.1 405.8 %reduce-scatter.4.cloned.1.call-start = ((), (), s32[]{:S(2)}) async-start(), calls=%async_computation.3 | async-start | bytes 4423680 | tf_op jit(solution)/shard_map/reduce_scatter | solution.py:64
  135.2 94.1 %collective-permute-start.13 = (bf16[768,960]{0,1:T(8,128)(2,1)}, bf16[768,960]{0,1:T(8,128)(2,1)}, u32[]{:S(2)}, u32[]{:S(2)}) collective-permute-start(bf16[768,960]{0,1:T(8,128)(2,1)} %copy.90), channel_id=1, source_target_pairs={{0,1},{1,0},{2,3},{3,2},{4,5},{5,4},{6,7},{7,6},{8,9},{9,8},{10,11... | collective-permute-start | bytes 4423688 | tf_op jit(solution)/shard_map/ppermute | solution.py:21
  180.4 37.7 %collective-permute-start.9 = (bf16[768,960]{0,1:T(8,128)(2,1)}, bf16[768,960]{0,1:T(8,128)(2,1)}, u32[]{:S(2)}, u32[]{:S(2)}) collective-permute-start(bf16[768,960]{0,1:T(8,128)(2,1)} %copy.85), channel_id=1, source_target_pairs={{0,1},{1,0},{2,3},{3,2},{4,5},{5,4},{6,7},{7,6},{8,9},{9,8},{10,11... | collective-permute-start | bytes 4423688 | tf_op jit(solution)/shard_map/ppermute | solution.py:21
  244.7 30.1 %collective-permute-start.14 = (bf16[768,960]{0,1:T(8,128)(2,1)S(1)}, bf16[768,960]{0,1:T(8,128)(2,1)S(1)}, u32[]{:S(2)}, u32[]{:S(2)}) collective-permute-start(bf16[768,960]{0,1:T(8,128)(2,1)S(1)} %add_convert_fusion.2), channel_id=1, source_target_pairs={{0,1},{1,0},{2,3},{3,2},{4,5},{5,4},{6,7},{7,6},{8,9},{9,8},{10,11... | collective-permute-start | bytes 4423688 | tf_op jit(solution)/shard_map/ppermute | solution.py:21
  248.1 144.1 %collective-permute-start.56 = (bf16[1280,480]{0,1:T(8,128)(2,1)}, bf16[1280,480]{0,1:T(8,128)(2,1)}, u32[]{:S(2)}, u32[]{:S(2)}) collective-permute-start(bf16[1280,480]{0,1:T(8,128)(2,1)} %fusion.26), channel_id=1, source_target_pairs={{0,2},{2,0},{1,3},{3,1},{4,6},{6,4},{5,7},{7,5},{8,10},{10,8},{9,1... | collective-permute-start | bytes 3686408 | tf_op jit(solution)/shard_map/ppermute | solution.py:21
  252.8 137.6 %collective-permute-start.55 = (bf16[1280,480]{0,1:T(8,128)(2,1)}, bf16[1280,480]{0,1:T(8,128)(2,1)}, u32[]{:S(2)}, u32[]{:S(2)}) collective-permute-start(bf16[1280,480]{0,1:T(8,128)(2,1)} %fusion.25), channel_id=1, source_target_pairs={{0,2},{2,0},{1,3},{3,1},{4,6},{6,4},{5,7},{7,5},{8,10},{10,8},{9,1... | collective-permute-start | bytes 3686408 | tf_op jit(solution)/shard_map/ppermute | solution.py:21
  258.2 129.6 %collective-permute-start.57 = (bf16[1280,480]{0,1:T(8,128)(2,1)}, bf16[1280,480]{0,1:T(8,128)(2,1)}, u32[]{:S(2)}, u32[]{:S(2)}) collective-permute-start(bf16[1280,480]{0,1:T(8,128)(2,1)} %fusion.27), channel_id=1, source_target_pairs={{0,2},{2,0},{1,3},{3,1},{4,6},{6,4},{5,7},{7,5},{8,10},{10,8},{9,1... | collective-permute-start | bytes 3686408 | tf_op jit(solution)/shard_map/ppermute | solution.py:21
  382.3 45.1 %collective-permute-start.15 = (bf16[6,256,640]{2,1,0:T(8,128)(2,1)}, bf16[6,256,640]{2,1,0:T(8,128)(2,1)}, u32[]{:S(2)}, u32[]{:S(2)}) collective-permute-start(bf16[6,256,640]{2,1,0:T(8,128)(2,1)} %pad_maximum_fusion.2), channel_id=1, source_target_pairs={{0,1},{1,0},{2,3},{3,2},{4,5},{5,4},{6,7},{7,6},{8,9},{9,8},{10,11... | collective-permute-start | bytes 5898248 | tf_op jit(solution)/shard_map/ppermute | solution.py:21
  405.3 205.9 %all-gather.5.cloned.1.call-start = ((), (), s32[]{:S(2)}) async-start(), calls=%async_computation.2 | async-start | bytes 4423680 | tf_op jit(solution)/shard_map/all_gather | solution.py:67
  432.6 44.1 %collective-permute-start.16 = (bf16[6,128,640]{2,1,0:T(8,128)(2,1)}, bf16[6,128,640]{2,1,0:T(8,128)(2,1)S(1)}, u32[]{:S(2)}, u32[]{:S(2)}) collective-permute-start(bf16[6,128,640]{2,1,0:T(8,128)(2,1)} %slice.241), channel_id=1, source_target_pairs={{0,2},{2,0},{1,3},{3,1},{4,6},{6,4},{5,7},{7,5},{8,10},{10,8},{9,1... | collective-permute-start | bytes 2949128 | tf_op jit(solution)/shard_map/ppermute | solution.py:21
  433.3 35.4 %collective-permute-start.29 = (bf16[30,1920]{1,0:T(8,128)(2,1)}, bf16[30,1920]{1,0:T(8,128)(2,1)}, u32[]{:S(2)}, u32[]{:S(2)}) collective-permute-start(bf16[30,1920]{1,0:T(8,128)(2,1)} %get-tuple-element.86), channel_id=1, source_target_pairs={{0,20},{4,16},{8,28},{12,24},{16,4},{20,0},{24,12},{28,8},{1,21},{... | collective-permute-start | bytes 345608 | tf_op jit(solution)/shard_map/ppermute | solution.py:72
  433.5 35.3 %collective-permute-start.28 = (bf16[30,1920]{1,0:T(8,128)(2,1)}, bf16[30,1920]{1,0:T(8,128)(2,1)}, u32[]{:S(2)}, u32[]{:S(2)}) collective-permute-start(bf16[30,1920]{1,0:T(8,128)(2,1)} %get-tuple-element.87), channel_id=1, source_target_pairs={{0,16},{4,20},{8,24},{12,28},{16,0},{20,4},{24,8},{28,12},{1,17},{... | collective-permute-start | bytes 345608 | tf_op jit(solution)/shard_map/ppermute | solution.py:72
  436.2 32.6 %collective-permute-start.27 = (bf16[30,1920]{1,0:T(8,128)(2,1)}, bf16[30,1920]{1,0:T(8,128)(2,1)}, u32[]{:S(2)}, u32[]{:S(2)}) collective-permute-start(bf16[30,1920]{1,0:T(8,128)(2,1)} %get-tuple-element.88), channel_id=1, source_target_pairs={{0,12},{4,8},{8,4},{12,0},{16,28},{20,24},{24,20},{28,16},{1,13},{... | collective-permute-start | bytes 345608 | tf_op jit(solution)/shard_map/ppermute | solution.py:72
  471.3 55.9 %collective-permute-start.37 = (bf16[30,1920]{1,0:T(8,128)(2,1)}, bf16[30,1920]{1,0:T(8,128)(2,1)}, u32[]{:S(2)}, u32[]{:S(2)}) collective-permute-start(bf16[30,1920]{1,0:T(8,128)(2,1)} %get-tuple-element.45), channel_id=1, source_target_pairs={{0,24},{4,28},{8,16},{12,20},{16,8},{20,12},{24,0},{28,4},{1,25},{... | collective-permute-start | bytes 345608 | tf_op jit(solution)/shard_map/ppermute | solution.py:72
  472.9 52.8 %collective-permute-start.36 = (bf16[30,1920]{1,0:T(8,128)(2,1)}, bf16[30,1920]{1,0:T(8,128)(2,1)}, u32[]{:S(2)}, u32[]{:S(2)}) collective-permute-start(bf16[30,1920]{1,0:T(8,128)(2,1)} %get-tuple-element.45), channel_id=1, source_target_pairs={{0,20},{4,16},{8,28},{12,24},{16,4},{20,0},{24,12},{28,8},{1,21},{... | collective-permute-start | bytes 345608 | tf_op jit(solution)/shard_map/ppermute | solution.py:72
  473.2 50.0 %collective-permute-start.35 = (bf16[30,1920]{1,0:T(8,128)(2,1)}, bf16[30,1920]{1,0:T(8,128)(2,1)}, u32[]{:S(2)}, u32[]{:S(2)}) collective-permute-start(bf16[30,1920]{1,0:T(8,128)(2,1)} %get-tuple-element.45), channel_id=1, source_target_pairs={{0,16},{4,20},{8,24},{12,28},{16,0},{20,4},{24,8},{28,12},{1,17},{... | collective-permute-start | bytes 345608 | tf_op jit(solution)/shard_map/ppermute | solution.py:72
  476.8 45.4 %collective-permute-start.34 = (bf16[30,1920]{1,0:T(8,128)(2,1)}, bf16[30,1920]{1,0:T(8,128)(2,1)}, u32[]{:S(2)}, u32[]{:S(2)}) collective-permute-start(bf16[30,1920]{1,0:T(8,128)(2,1)} %get-tuple-element.45), channel_id=1, source_target_pairs={{0,12},{4,8},{8,4},{12,0},{16,28},{20,24},{24,20},{28,16},{1,13},{... | collective-permute-start | bytes 345608 | tf_op jit(solution)/shard_map/ppermute | solution.py:72
  523.2 64.4 %collective-permute-start.11 = (bf16[6,128,480]{1,2,0:T(8,128)(2,1)}, bf16[6,128,480]{1,2,0:T(8,128)(2,1)}, u32[]{:S(2)}, u32[]{:S(2)}) collective-permute-start(bf16[6,128,480]{1,2,0:T(8,128)(2,1)} %get-tuple-element.66), channel_id=1, source_target_pairs={{0,2},{2,0},{1,3},{3,1},{4,6},{6,4},{5,7},{7,5},{8,10},{10,8},{9,1... | collective-permute-start | bytes 2211848 | tf_op jit(solution)/shard_map/ppermute | solution.py:21
  525.7 47.2 %collective-permute-start.17 = (bf16[6,128,480]{1,2,0:T(8,128)(2,1)}, bf16[6,128,480]{1,2,0:T(8,128)(2,1)}, u32[]{:S(2)}, u32[]{:S(2)}) collective-permute-start(bf16[6,128,480]{1,2,0:T(8,128)(2,1)} %get-tuple-element.62), channel_id=1, source_target_pairs={{0,2},{2,0},{1,3},{3,1},{4,6},{6,4},{5,7},{7,5},{8,10},{10,8},{9,1... | collective-permute-start | bytes 2211848 | tf_op jit(solution)/shard_map/ppermute | solution.py:21
  530.4 34.4 %collective-permute-start.40 = (bf16[240,640]{1,0:T(8,128)(2,1)}, bf16[240,640]{1,0:T(8,128)(2,1)}, u32[]{:S(2)}, u32[]{:S(2)}) collective-permute-start(bf16[240,640]{1,0:T(8,128)(2,1)} %fusion.81), channel_id=1, source_target_pairs={{0,2},{2,0},{1,3},{3,1},{4,6},{6,4},{5,7},{7,5},{8,10},{10,8},{9,1... | collective-permute-start | bytes 921608 | tf_op jit(solution)/shard_map/ppermute | solution.py:21
  (105 other events, 1248.0 us)
Sparse Core Ops, SparseCore 0:
  112.2 71.4 all-gather.2
  405.4 112.4 reduce-scatter.3
  520.3 80.3 all-gather.4

commit v3 on v2

--- a/solution.py
+++ b/solution.py
@@ -325,6 +325,8 @@
     grad_probs = dot("sqhgd,skhd->shgqk", grad_att_grp, value_rows)
     row_delta = jnp.sum(exact_probs * grad_probs, axis=-1, keepdims=True)
     grad_scores = (exact_probs * (grad_probs - row_delta)).astype(bf16)
+    grad_scores, ffn_part = lax.optimization_barrier((grad_scores, ffn_part))
+    ffn_piece = lax.psum_scatter(ffn_part, "dp", scatter_dimension=0, tiled=True)
     grad_keys = dot("shgqk,sqhgd->skhd", grad_scores, query_grp) * HD ** (-0.5)
     grad_values = dot("shgqk,sqhgd->skhd", exact_probs.astype(bf16), grad_att_grp)
     grad_kv = jnp.concatenate(
@@ -350,6 +352,7 @@
         .astype(bf16)
     )
     grad_kv_lin = jnp.concatenate([grad_key_lin, grad_kv_own[..., KD:].astype(bf16)], axis=2)
+    grad_kv_lin, ffn_piece = lax.optimization_barrier((grad_kv_lin, ffn_piece))
     query_part = dot("sqd,sqe->de", first_tok, grad_query_lin)
     kv_part = dot("sqd,sqe->de", first_tok, grad_kv_lin)
     grad_first = dot("sqe,de->sqd", grad_query_lin, qkv_full[:, :QD]) + dot(
@@ -361,7 +364,7 @@
         jnp.float32
     )
 
-    ffn_sum = dp_total(ffn_part, 0).astype(jnp.float32)
+    ffn_sum = lax.all_gather(ffn_piece, "dp", axis=0, tiled=True).astype(jnp.float32)
     qo_part = jnp.concatenate([query_part, output_part], axis=1)
     qo_sum = dp_direct(scatter_rows(qo_part, row_index, col_index)).astype(jnp.float32)
     kv_grad = dp_direct(scatter_rows(kv_part, row_index, col_index)).astype(jnp.float32)

time: 646 us -> 613 us (0.949)
  other arithmetic: 117 us -> 91.9 us
  local copies, waits for them, and re-layouts: 113 us -> 98.9 us
  waiting for transfers between devices: 122 us -> 135 us
  starting transfers between devices: 91 us -> 82.2 us
    sub x0 -> x1, matrix products: none -> 25.7 us  [local(): grad_scores = (exact_probs * (grad_probs - row_delta)).astype(bf16)]
    dot_general x37 -> x36, matrix products: 169 us -> 144 us  [dot(): return jnp.einsum(spec, left, right, preferred_element_type=jnp.float32)]
    convert_element_type x2 -> x1, other arithmetic: 23.6 us -> 3.23 us  [local(): lax.all_gather(ffn_piece, 'dp', axis=0, tiled=True).astype(jnp.float32)]
    unnamed x3 -> x4, waiting for transfers between devices: 0.05 us -> 14.3 us
    ppermute x31, waiting for transfers between devices: 18.5 us -> 30.4 us  [xor_partner(): return lax.ppermute(values, 'dp', [(i, i ^ step) for i in range(size)])]
    ppermute x31, starting transfers between devices: 68.7 us -> 58.9 us  [xor_partner(): return lax.ppermute(values, 'dp', [(i, i ^ step) for i in range(size)])]
    ppermute x27, waiting for transfers between devices: 98.3 us -> 90.6 us  [swap(): lax.ppermute(values, axis_name, [(i, size - 1 - i) for i in range(size)])]
    reshape x2 -> x0, local copies, waits for them, and re-layouts: 6.74 us -> none  [the longest x1 4.13 us: local(): grad_values.reshape(seq_count, length, KD)]
  transfers between devices with their start and end apart: 61 -> 61, of which waited for: 18 -> 25; matrix products, arithmetic and copies ran while one was open for 55% -> 49% of each run, Pallas kernels for 0% -> 0%
where the time goes in v3:
time: 613 us; the launch traced here: 604 us
  matrix products  180 us (29%)
  waiting for transfers between devices  135 us (22%)
  local copies, waits for them, and re-layouts  98.9 us (16%)
  other arithmetic  91.9 us (15%)
  starting transfers between devices  82.2 us (13%)
  between operations  15.4 us (3%)
    dot_general x36, matrix products, dot(): return jnp.einsum(spec, left, right, preferred_element_type=jnp.float32)  144 us
    ppermute x27, waiting for transfers between devices, swap(): lax.ppermute(values, axis_name, [(i, size - 1 - i) for i in range(size)])  90.6 us
    ppermute x31, starting transfers between devices, xor_partner(): return lax.ppermute(values, 'dp', [(i, i ^ step) for i in range(size)])  58.9 us
    unnamed x174, local copies, waits for them, and re-layouts  39.6 us
    ppermute x31, waiting for transfers between devices, xor_partner(): return lax.ppermute(values, 'dp', [(i, i ^ step) for i in range(size)])  30.4 us
    select_n x11, other arithmetic, ordered(): jnp.where(index == 0, jnp.concatenate([own, other], axis=axis), jnp.conca...  30.2 us
    sub x1, matrix products, local(): grad_scores = (exact_probs * (grad_probs - row_delta)).astype(bf16)  25.7 us
    ppermute x27, starting transfers between devices, swap(): lax.ppermute(values, axis_name, [(i, size - 1 - i) for i in range(size)])  22.9 us
  transfers between devices with their start and end apart: 61, of which 25 were waited for; matrix products, arithmetic and copies ran while one was open for 49% of the time, Pallas kernels for 0%

profile of v3, /device:TPU:0, one launch (start us, length us, event | category | flops | bytes accessed | tf_op | source)
XLA Modules:
  0.0 603.9 jit_solution(15999251892921250138)
XLA Ops:
  24.8 7.5 %collective-permute-done.3 = bf16[240,1600]{1,0:T(8,128)(2,1)S(1)} collective-permute-done((bf16[240,1600]{1,0:T(8,128)(2,1)S(1)}, bf16[240,1600]{1,0:T(8,128)(2,1)S(1)}, u32[]{:S(2)}, u32[]{:S(2)}) %collective-permute-start.3) | collective-permute-done | bytes 768032 | tf_op jit(solution)/shard_map/ppermute | solution.py:21
  35.1 23.0 %collective-permute-done.2 = f32[2,480]{1,0:T(2,128)S(1)} collective-permute-done((f32[2,480]{1,0:T(2,128)S(1)}, f32[2,480]{1,0:T(2,128)S(1)}, u32[]{:S(2)}, u32[]{:S(2)}) %collective-permute-start.2) | collective-permute-done | bytes 3872 | tf_op jit(solution)/shard_map/ppermute | solution.py:21
  72.5 20.7 %collective-permute-done.5 = bf16[6,128,640]{1,2,0:T(8,128)(2,1)S(1)} collective-permute-done((bf16[6,128,640]{1,2,0:T(8,128)(2,1)S(1)}, bf16[6,128,640]{1,2,0:T(8,128)(2,1)S(1)}, u32[]{:S(2)}, u32[]{:S(2)}) %collective-permute-start.5) | collective-permute-done | bytes 983072 | tf_op jit(solution)/shard_map/ppermute | solution.py:21
  102.5 8.1 %collective-permute-done.7 = bf16[240,960]{1,0:T(8,128)(2,1)S(1)} collective-permute-done((bf16[240,960]{1,0:T(8,128)(2,1)}, bf16[240,960]{1,0:T(8,128)(2,1)S(1)}, u32[]{:S(2)}, u32[]{:S(2)}) %collective-permute-start.7) | collective-permute-done | bytes 460832 | tf_op jit(solution)/shard_map/ppermute | solution.py:21
  142.4 10.1 %fusion.11 = (f32[6,5,3,128]{3,2,1,0:T(4,128)S(1)}, f32[6,5,512,128,3]{3,2,4,1,0:T(8,128)}) fusion(pred[6,128,512]{1,2,0:T(8,128)(4,1)S(1)} %copy-done.21, bf16[6,512,5,64,1]{1,3,4,2,0:T(8,128)(2,1)S(1)} %bitcast.300, bf16[6,128,5,3,32]{1,4,3,2,0:T(8,128)(2,1)S(1)} %bitcast.312, bf16[6,128,5,3,32]{1,4,3,2,0:T(8,128)(2,1)S(1)} %bitcast.310), kind=kOutput, calls=%fused_computation.16 | convolution fusion | flops 775607040 | bytes 27472896 | tf_op jit(solution)/shard_map/sqhgd,skhd->shgqk/dot_general | solution.py:153
  152.5 10.5 %fusion.5 = f32[6,5,3,128]{3,2,1,0:T(4,128)S(1)} fusion(f32[6,5,3,128]{3,2,1,0:T(4,128)S(1)} %get-tuple-element.129, f32[6,5,512,128,3]{3,2,4,1,0:T(8,128)} %get-tuple-element.130, pred[6,128,512]{1,2,0:T(8,128)(4,1)S(1)} %copy-done.21), kind=kLoop, calls=%fused_computation.11 | loop fusion | flops 23581440 | bytes 24078336 | tf_op jit(solution)/shard_map/reduce_sum | solution.py:259
  163.1 11.2 %fusion.51 = bf16[6,5,64,3,128]{4,2,3,1,0:T(8,128)(2,1)S(1)} fusion(bf16[6,512,5,64,1]{1,3,4,2,0:T(8,128)(2,1)S(1)} %bitcast.342, f32[6,5,3,128]{3,2,1,0:T(4,128)S(1)} %fusion.5, f32[6,5,3,128]{3,2,1,0:T(4,128)S(1)} %get-tuple-element.129, f32[6,5,512,128,3]{3,2,4,1,0:T(8,128)} %get-tuple-element.130, pred[6,128,512]{1,2,0:T(8,128)(4,1)S(1)} %copy-done.21), kind=kOutput, calls=%fused_computation.113 | convolution fusion | flops 785203200 | bytes 27518976 | tf_op jit(solution)/shard_map/shgqk,skhd->sqhgd/dot_general | solution.py:123
  184.6 12.8 %maximum_select_fusion = bf16[3,1280,960]{2,1,0:T(8,128)(2,1)S(1)} fusion(bf16[3,1280,480]{2,1,0:T(8,128)(2,1)} %all-gather.3.cloned.1.call-done, bf16[1,1280,480]{2,1,0:T(8,128)(2,1)} %bitcast.323, bf16[1,1280,480]{2,1,0:T(8,128)(2,1)} %bitcast.322, bf16[1,1280,480]{2,1,0:T(8,128)(2,1)} %bitcast.321, pred[]{:T(512)S(6)} %eq.14), kind=kLoop, calls=%fused_computation.17 | loop fusion | flops 62668800 | bytes 14745601 | tf_op jit(solution)/shard_map/jit(_where)/select_n | solution.py:25
  203.9 5.8 multiply_convert_fusion.2
  217.1 5.5 fusion.45
  222.7 5.6 fusion.41
  228.3 8.0 %multiply_convert_fusion = (bf16[768,1280]{1,0:T(8,128)(2,1)}, bf16[768,1280]{1,0:T(8,128)(2,1)}, bf16[768,1280]{1,0:T(8,128)(2,1)S(1)}) fusion(f32[768,1280]{1,0:T(8,128)} %fusion.41, f32[768,1280]{1,0:T(8,128)} %fusion.45, bf16[768,960]{0,1:T(8,128)(2,1)} %collective-permute-done.13, bf16[3,1280,960]{2,1,0:T(8,128)(2,1)S(1)} %maximum_select_fusion), kind=kOutput, calls=%fused_computation.32 | convolution fusion | flops 1903165440 | bytes 17858560 | tf_op jit(solution)/shard_map/td,fd->tf/dot_general | solution.py:123
  236.3 6.0 fusion.39
  287.3 7.2 %fusion.116 = (bf16[6,128,960]{1,2,0:T(8,128)(2,1)S(1)}, f32[6,128,960]{1,2,0:T(8,128)}) fusion(f32[6,128,960]{1,2,0:T(8,128)} %copy.90, bf16[6,128,960]{1,2,0:T(8,128)(2,1)S(1)} %copy-done.19, bf16[6,128,960]{1,2,0:T(8,128)(2,1)S(1)} %maximum_select_fusion.6, f32[960]{0:T(1024)S(1)} %bitcast.364, f32[6,128]{1,0:T(8,128)S(1)} %get-tuple-element.127, ...), kind=kOutput, calls=%fused_computation.296 | output fusion | flops 19171008 | bytes 11806465 | tf_op jit(solution)/shard_map/mul | solution.py:117
  297.3 25.7 %fusion.4 = bf16[6,5,3,128,512]{3,4,2,1,0:T(8,128)(2,1)} fusion(f32[6,5,3,128]{3,2,1,0:T(4,128)S(1)} %copy-done.46, f32[6,5,512,128,3]{3,2,4,1,0:T(8,128)} %get-tuple-element.130, pred[6,128,512]{1,2,0:T(8,128)(4,1)S(1)} %copy-done.21, bf16[6,512,5,64,1]{1,3,4,2,0:T(8,128)(2,1)} %bitcast.343, bf16[6,128,5,3,64]{1,4,3,2,0:T(8,128)(2,1)} %bitcast.377), kind=kOutput, calls=%fused_computation.6 | convolution fusion | flops 1568943872 | bytes 39269376 | tf_op jit(solution)/shard_map/sub | solution.py:327
  350.9 8.4 %fusion.13 = bf16[6,5,64,512]{3,2,1,0:T(8,128)(2,1)S(1)} fusion(bf16[6,5,3,128,512]{3,4,2,1,0:T(8,128)(2,1)} %fusion.4, bf16[6,128,5,3,32]{1,4,3,2,0:T(8,128)(2,1)S(1)} %bitcast.313, bf16[6,128,5,3,32]{1,4,3,2,0:T(8,128)(2,1)S(1)} %bitcast.311), kind=kOutput, calls=%fused_computation.30 | convolution fusion | flops 759889920 | bytes 15237120 | tf_op jit(solution)/shard_map/shgqk,sqhgd->skhd/dot_general | solution.py:123
  359.3 11.4 %bitcast_convert_fusion = bf16[6,5,64,512]{3,2,1,0:T(8,128)(2,1)S(1)} fusion(bf16[6,128,5,3,64]{1,4,3,2,0:T(8,128)(2,1)} %bitcast.378, f32[6,5,3,128]{3,2,1,0:T(4,128)S(1)} %copy-done.47, f32[6,5,512,128,3]{3,2,4,1,0:T(8,128)} %get-tuple-element.130, pred[6,128,512]{1,2,0:T(8,128)(4,1)} %compare_and_fusion), kind=kOutput, calls=%fused_computation.28 | convolution fusion | flops 779550720 | bytes 27472896 | tf_op jit(solution)/shard_map/shgqk,sqhgd->skhd/dot_general | solution.py:123
  379.4 6.1 %copy.121 = bf16[3840,480]{1,0:T(8,128)(2,1)} copy(bf16[3840,480]{0,1:T(8,128)(2,1)} %pad_maximum_fusion.1) | data formatting | bytes 7372800
  385.5 5.6 fusion.52
  391.1 9.5 %collective-permute-done.27 = bf16[240,1920]{1,0:T(8,128)(2,1)} collective-permute-done((bf16[240,1920]{1,0:T(8,128)(2,1)}, bf16[240,1920]{1,0:T(8,128)(2,1)}, u32[]{:S(2)}, u32[]{:S(2)}) %collective-permute-start.27) | collective-permute-done | bytes 921632 | tf_op jit(solution)/shard_map/ppermute | solution.py:21
  430.2 6.0 fusion.53
  448.7 5.7 collective-permute-start.36
  481.9 14.3 %reduce-scatter.4.cloned.1.call-done = bf16[480,480]{1,0:T(8,128)(2,1)} async-done(((bf16[3840,480]{1,0:T(8,128)(2,1)}), bf16[480,480]{1,0:T(8,128)(2,1)}) %reduce-scatter.4.cloned.1.call-update) | async-done | bytes 460816
  525.1 14.3 %collective-permute-done.43 = bf16[240,640]{1,0:T(8,128)(2,1)S(1)} collective-permute-done((bf16[240,640]{1,0:T(8,128)(2,1)S(1)}, bf16[240,640]{1,0:T(8,128)(2,1)S(1)}, u32[]{:S(2)}, u32[]{:S(2)}) %collective-permute-start.43) | collective-permute-done | bytes 307232 | tf_op jit(solution)/shard_map/ppermute | solution.py:21
  (433 shorter events, 339.5 us)
Async XLA Ops:
  7.2 177.5 %all-gather.3.cloned.1.call-start = ((), (), s32[]{:S(2)}) async-start(), calls=%async_computation.1 | async-start | bytes 4423680 | tf_op jit(solution)/shard_map/all_gather | solution.py:208
  15.1 43.6 %collective-permute-start = (bf16[6,128,480]{1,2,0:T(8,128)(2,1)}, bf16[6,128,480]{1,2,0:T(8,128)(2,1)}, u32[]{:S(2)}, u32[]{:S(2)}) collective-permute-start(bf16[6,128,480]{1,2,0:T(8,128)(2,1)} %get-tuple-element.76), channel_id=1, source_target_pairs={{0,2},{2,0},{1,3},{3,1},{4,6},{6,4},{5,7},{7,5},{8,10},{10,8},{9,1... | collective-permute-start | bytes 2211848 | tf_op jit(solution)/shard_map/ppermute | solution.py:21
  22.7 38.2 %collective-permute-start.1 = (bf16[3,160,480]{2,1,0:T(8,128)(2,1)}, bf16[3,160,480]{2,1,0:T(8,128)(2,1)}, u32[]{:S(2)}, u32[]{:S(2)}) collective-permute-start(bf16[3,160,480]{2,1,0:T(8,128)(2,1)} %pad_maximum_fusion.10), channel_id=1, source_target_pairs={{0,2},{2,0},{1,3},{3,1},{4,6},{6,4},{5,7},{7,5},{8,10},{10,8},{9,1... | collective-permute-start | bytes 1382408 | tf_op jit(solution)/shard_map/ppermute | solution.py:21
  24.7 33.3 %collective-permute-start.2 = (f32[2,480]{1,0:T(2,128)S(1)}, f32[2,480]{1,0:T(2,128)S(1)}, u32[]{:S(2)}, u32[]{:S(2)}) collective-permute-start(f32[2,480]{1,0:T(2,128)S(1)} %pad_maximum_fusion.13), channel_id=1, source_target_pairs={{0,2},{2,0},{1,3},{3,1},{4,6},{6,4},{5,7},{7,5},{8,10},{10,8},{9,1... | collective-permute-start | bytes 11528 | tf_op jit(solution)/shard_map/ppermute | solution.py:21
  33.9 28.3 %collective-permute-start.4 = (bf16[2,240,1600]{2,1,0:T(8,128)(2,1)}, bf16[2,240,1600]{2,1,0:T(8,128)(2,1)}, u32[]{:S(2)}, u32[]{:S(2)}) collective-permute-start(bf16[2,240,1600]{2,1,0:T(8,128)(2,1)} %maximum_select_fusion.4), channel_id=1, source_target_pairs={{0,1},{1,0},{2,3},{3,2},{4,5},{5,4},{6,7},{7,6},{8,9},{9,8},{10,11... | collective-permute-start | bytes 4608008 | tf_op jit(solution)/shard_map/ppermute | solution.py:21
  70.2 23.1 %collective-permute-start.5 = (bf16[6,128,640]{1,2,0:T(8,128)(2,1)S(1)}, bf16[6,128,640]{1,2,0:T(8,128)(2,1)S(1)}, u32[]{:S(2)}, u32[]{:S(2)}) collective-permute-start(bf16[6,128,640]{1,2,0:T(8,128)(2,1)S(1)} %pad_maximum_fusion.6), channel_id=1, source_target_pairs={{0,2},{2,0},{1,3},{3,1},{4,6},{6,4},{5,7},{7,5},{8,10},{10,8},{9,1... | collective-permute-start | bytes 2949128 | tf_op jit(solution)/shard_map/ppermute | solution.py:21
  93.4 44.5 %collective-permute-start.6 = (bf16[6,256,640]{1,2,0:T(8,128)(2,1)S(1)}, bf16[6,256,640]{1,2,0:T(8,128)(2,1)}, u32[]{:S(2)}, u32[]{:S(2)}) collective-permute-start(bf16[6,256,640]{1,2,0:T(8,128)(2,1)S(1)} %pad_maximum_fusion.3), channel_id=1, source_target_pairs={{0,1},{1,0},{2,3},{3,2},{4,5},{5,4},{6,7},{7,6},{8,9},{9,8},{10,11... | collective-permute-start | bytes 5898248 | tf_op jit(solution)/shard_map/ppermute | solution.py:21
  101.9 24.3 %collective-permute-start.12 = (bf16[6,128,480]{1,2,0:T(8,128)(2,1)}, bf16[6,128,480]{1,2,0:T(8,128)(2,1)}, u32[]{:S(2)}, u32[]{:S(2)}) collective-permute-start(bf16[6,128,480]{1,2,0:T(8,128)(2,1)} %get-tuple-element.72), channel_id=1, source_target_pairs={{0,2},{2,0},{1,3},{3,1},{4,6},{6,4},{5,7},{7,5},{8,10},{10,8},{9,1... | collective-permute-start | bytes 2211848 | tf_op jit(solution)/shard_map/ppermute | solution.py:21
  111.8 23.5 %collective-permute-start.8 = (bf16[2,240,960]{2,1,0:T(8,128)(2,1)}, bf16[2,240,960]{2,1,0:T(8,128)(2,1)}, u32[]{:S(2)}, u32[]{:S(2)}) collective-permute-start(bf16[2,240,960]{2,1,0:T(8,128)(2,1)} %maximum_select_fusion.11), channel_id=1, source_target_pairs={{0,1},{1,0},{2,3},{3,2},{4,5},{5,4},{6,7},{7,6},{8,9},{9,8},{10,11... | collective-permute-start | bytes 2764808 | tf_op jit(solution)/shard_map/ppermute | solution.py:21
  113.1 383.0 %reduce-scatter.4.cloned.1.call-start = ((), (), s32[]{:S(2)}) async-start(), calls=%async_computation.3 | async-start | bytes 4423680
  135.3 93.0 %collective-permute-start.13 = (bf16[768,960]{0,1:T(8,128)(2,1)}, bf16[768,960]{0,1:T(8,128)(2,1)}, u32[]{:S(2)}, u32[]{:S(2)}) collective-permute-start(bf16[768,960]{0,1:T(8,128)(2,1)} %copy.88), channel_id=1, source_target_pairs={{0,1},{1,0},{2,3},{3,2},{4,5},{5,4},{6,7},{7,6},{8,9},{9,8},{10,11... | collective-permute-start | bytes 4423688 | tf_op jit(solution)/shard_map/ppermute | solution.py:21
  182.4 34.8 %collective-permute-start.9 = (bf16[768,960]{0,1:T(8,128)(2,1)}, bf16[768,960]{0,1:T(8,128)(2,1)}, u32[]{:S(2)}, u32[]{:S(2)}) collective-permute-start(bf16[768,960]{0,1:T(8,128)(2,1)} %copy.83), channel_id=1, source_target_pairs={{0,1},{1,0},{2,3},{3,2},{4,5},{5,4},{6,7},{7,6},{8,9},{9,8},{10,11... | collective-permute-start | bytes 4423688 | tf_op jit(solution)/shard_map/ppermute | solution.py:21
  247.1 29.1 %collective-permute-start.14 = (bf16[768,960]{0,1:T(8,128)(2,1)S(1)}, bf16[768,960]{0,1:T(8,128)(2,1)S(1)}, u32[]{:S(2)}, u32[]{:S(2)}) collective-permute-start(bf16[768,960]{0,1:T(8,128)(2,1)S(1)} %add_convert_fusion.2), channel_id=1, source_target_pairs={{0,1},{1,0},{2,3},{3,2},{4,5},{5,4},{6,7},{7,6},{8,9},{9,8},{10,11... | collective-permute-start | bytes 4423688 | tf_op jit(solution)/shard_map/ppermute | solution.py:21
  250.6 75.8 %collective-permute-start.15 = (bf16[1280,480]{0,1:T(8,128)(2,1)}, bf16[1280,480]{0,1:T(8,128)(2,1)}, u32[]{:S(2)}, u32[]{:S(2)}) collective-permute-start(bf16[1280,480]{0,1:T(8,128)(2,1)} %fusion.26), channel_id=1, source_target_pairs={{0,2},{2,0},{1,3},{3,1},{4,6},{6,4},{5,7},{7,5},{8,10},{10,8},{9,1... | collective-permute-start | bytes 3686408 | tf_op jit(solution)/shard_map/ppermute | solution.py:21
  255.4 72.9 %collective-permute-start.16 = (bf16[1280,480]{0,1:T(8,128)(2,1)}, bf16[1280,480]{0,1:T(8,128)(2,1)}, u32[]{:S(2)}, u32[]{:S(2)}) collective-permute-start(bf16[1280,480]{0,1:T(8,128)(2,1)} %fusion.27), channel_id=1, source_target_pairs={{0,2},{2,0},{1,3},{3,1},{4,6},{6,4},{5,7},{7,5},{8,10},{10,8},{9,1... | collective-permute-start | bytes 3686408 | tf_op jit(solution)/shard_map/ppermute | solution.py:21
  259.2 73.6 %collective-permute-start.17 = (bf16[1280,480]{0,1:T(8,128)(2,1)}, bf16[1280,480]{0,1:T(8,128)(2,1)}, u32[]{:S(2)}, u32[]{:S(2)}) collective-permute-start(bf16[1280,480]{0,1:T(8,128)(2,1)} %fusion.28), channel_id=1, source_target_pairs={{0,2},{2,0},{1,3},{3,1},{4,6},{6,4},{5,7},{7,5},{8,10},{10,8},{9,1... | collective-permute-start | bytes 3686408 | tf_op jit(solution)/shard_map/ppermute | solution.py:21
  372.6 34.5 %collective-permute-start.18 = (bf16[6,256,640]{1,2,0:T(8,128)(2,1)}, bf16[6,256,640]{1,2,0:T(8,128)(2,1)}, u32[]{:S(2)}, u32[]{:S(2)}) collective-permute-start(bf16[6,256,640]{1,2,0:T(8,128)(2,1)} %pad_maximum_fusion.2), channel_id=1, source_target_pairs={{0,1},{1,0},{2,3},{3,2},{4,5},{5,4},{6,7},{7,6},{8,9},{9,8},{10,11... | collective-permute-start | bytes 5898248 | tf_op jit(solution)/shard_map/ppermute | solution.py:21
  385.5 197.4 %all-gather.5.cloned.1.call-start = ((), (), s32[]{:S(2)}) async-start(), calls=%async_computation.2 | async-start | bytes 4423680 | tf_op jit(solution)/shard_map/all_gather | solution.py:367
  412.4 45.8 %collective-permute-start.19 = (bf16[6,128,640]{1,2,0:T(8,128)(2,1)}, bf16[6,128,640]{1,2,0:T(8,128)(2,1)}, u32[]{:S(2)}, u32[]{:S(2)}) collective-permute-start(bf16[6,128,640]{1,2,0:T(8,128)(2,1)} %slice.241), channel_id=1, source_target_pairs={{0,2},{2,0},{1,3},{3,1},{4,6},{6,4},{5,7},{7,5},{8,10},{10,8},{9,1... | collective-permute-start | bytes 2949128 | tf_op jit(solution)/shard_map/ppermute | solution.py:21
  413.9 29.4 %collective-permute-start.31 = (bf16[30,1920]{1,0:T(8,128)(2,1)}, bf16[30,1920]{1,0:T(8,128)(2,1)S(1)}, u32[]{:S(2)}, u32[]{:S(2)}) collective-permute-start(bf16[30,1920]{1,0:T(8,128)(2,1)} %get-tuple-element.95), channel_id=1, source_target_pairs={{0,16},{4,20},{8,24},{12,28},{16,0},{20,4},{24,8},{28,12},{1,17},{... | collective-permute-start | bytes 345608 | tf_op jit(solution)/shard_map/ppermute | solution.py:72
  416.4 31.0 %collective-permute-start.32 = (bf16[30,1920]{1,0:T(8,128)(2,1)}, bf16[30,1920]{1,0:T(8,128)(2,1)S(1)}, u32[]{:S(2)}, u32[]{:S(2)}) collective-permute-start(bf16[30,1920]{1,0:T(8,128)(2,1)} %get-tuple-element.94), channel_id=1, source_target_pairs={{0,20},{4,16},{8,28},{12,24},{16,4},{20,0},{24,12},{28,8},{1,21},{... | collective-permute-start | bytes 345608 | tf_op jit(solution)/shard_map/ppermute | solution.py:72
  419.4 28.0 %collective-permute-start.33 = (bf16[30,1920]{1,0:T(8,128)(2,1)}, bf16[30,1920]{1,0:T(8,128)(2,1)S(1)}, u32[]{:S(2)}, u32[]{:S(2)}) collective-permute-start(bf16[30,1920]{1,0:T(8,128)(2,1)} %get-tuple-element.93), channel_id=1, source_target_pairs={{0,24},{4,28},{8,16},{12,20},{16,8},{20,12},{24,0},{28,4},{1,25},{... | collective-permute-start | bytes 345608 | tf_op jit(solution)/shard_map/ppermute | solution.py:72
  513.4 30.3 %collective-permute-start.20 = (bf16[6,128,480]{1,2,0:T(8,128)(2,1)S(1)}, bf16[6,128,480]{1,2,0:T(8,128)(2,1)S(1)}, u32[]{:S(2)}, u32[]{:S(2)}) collective-permute-start(bf16[6,128,480]{1,2,0:T(8,128)(2,1)S(1)} %get-tuple-element.70), channel_id=1, source_target_pairs={{0,2},{2,0},{1,3},{3,1},{4,6},{6,4},{5,7},{7,5},{8,10},{10,8},{9,1... | collective-permute-start | bytes 2211848 | tf_op jit(solution)/shard_map/ppermute | solution.py:21
  521.6 38.5 %collective-permute-start.11 = (bf16[6,128,480]{1,2,0:T(8,128)(2,1)S(1)}, bf16[6,128,480]{1,2,0:T(8,128)(2,1)S(1)}, u32[]{:S(2)}, u32[]{:S(2)}) collective-permute-start(bf16[6,128,480]{1,2,0:T(8,128)(2,1)S(1)} %get-tuple-element.74), channel_id=1, source_target_pairs={{0,2},{2,0},{1,3},{3,1},{4,6},{6,4},{5,7},{7,5},{8,10},{10,8},{9,1... | collective-permute-start | bytes 2211848 | tf_op jit(solution)/shard_map/ppermute | solution.py:21
  (114 other events, 1105.0 us)
Sparse Core Ops, SparseCore 0:
  113.2 71.3 all-gather.2
  385.6 110.4 reduce-scatter.3
  499.1 80.4 all-gather.4
